TPU v7x, 128 devices: a whole 4x4x4 slice. The times are simulated.
128 devices in a mesh: ctx: 16 (over x_lo, y, core), exp: 8 (over x_hi, z).
Axes of the slice: x: 4 (x_hi: 2, x_lo: 2; x = x_hi * 2 + x_lo), y: 4, z: 4, core: 2. Of those that a mesh axis runs over, the one named last changes fastest.
Arguments:
- queries: bfloat16 [2048, 4096], P('ctx', 'exp'), may hold values from -8 to 8
- new_keys: bfloat16 [2048, 1024], P('ctx', 'exp'), may hold values from -6 to 6
- new_values: bfloat16 [2048, 1024], P('ctx', 'exp'), may hold values from -6 to 6
- cache_keys: bfloat16 [16384, 1024], P('ctx', 'exp'), may hold values from -8 to 8
- cache_values: bfloat16 [16384, 1024], P('ctx', 'exp'), may hold values from -6 to 6
- cache_length: int32 [1], replicated, may hold values from 12288 to 16384
- residual: bfloat16 [2048, 4096], P(('ctx', 'exp')), may hold values from -6 to 6
- out_weight: bfloat16 [4096, 4096], P('exp'), may hold values from -0.5 to 0.5
- norm_gain: bfloat16 [4096], replicated, may hold values from 0.5 to 1.5
- route_ids: int32 [2048, 2], P('ctx'), may hold values from 0 to 7, all different within a row; in each aligned block of 128 rows (0 to 127, 128 to 255, ...) at most 48 rows name the same one
- route_gates: float32 [2048, 2], P('ctx'), may hold values from 0.2 to 1
- w_gate: bfloat16 [8, 4096, 14336], P('exp', None, 'ctx'), may hold values from -0.09375 to 0.09375
- w_up: bfloat16 [8, 4096, 14336], P('exp', None, 'ctx'), may hold values from -0.09375 to 0.09375
- w_down: bfloat16 [8, 14336, 4096], P('exp', 'ctx'), may hold values from -0.046875 to 0.046875
Outputs:
- layer_out: bfloat16 [2048, 4096], P(('ctx', 'exp'))
Inputs may be any that keep to these rules, and one draw needn't show every extreme that they name: `route_ids`: each row names 2 different experts; in each aligned block of 128 rows no expert is named more than 48 times, and in some block one expert is named exactly 48 times.
All inputs are finite; a program needn't handle non-finite values.
Results may differ from a plain program's by a relative error of at most 0.024.
Values may be sent and summed in bfloat16 or wider, within the bound.
A program may use at most 128 MiB of HBM per device.

v0:
```python
import math

import jax
import jax.numpy as jnp
from jax import lax
from jax.sharding import PartitionSpec as P

HD = 128


NEG = -1e30
EPS = 1e-05
BLOCK_ROWS = 1024


def attend_piece(
    carry,
    query_block,
    query_index,
    key_piece,
    value_piece,
    start,
    cache_rows,
    new_rows,
    cache_limit,
):
    shard_rows = cache_rows + new_rows
    kv_local = key_piece.shape[1] // HD
    group = query_block.shape[1] // key_piece.shape[1]
    heads_q = query_block.reshape(query_block.shape[0], kv_local, group, HD)
    count = key_piece.shape[0]
    width = min(count, BLOCK_ROWS)
    blocks = -(-count // width)
    keys_padded = key_piece.reshape(blocks, width, kv_local, HD)
    values_padded = value_piece.reshape(blocks, width, kv_local, HD)
    block_start = width * jnp.arange(blocks, dtype=jnp.int32)
    scale = 1.0 / math.sqrt(HD)

    def step_block(state, inputs):
        top, total, summed = state
        keys_block, values_block, first_row = inputs
        row_index = first_row + jnp.arange(width, dtype=jnp.int32)
        shard = row_index // shard_rows
        offset = row_index % shard_rows
        cache_pos = shard * cache_rows + offset
        new_pos = shard * new_rows + offset - cache_rows
        visible = jnp.where(
            (offset < cache_rows)[None, :],
            (cache_pos < cache_limit)[None, :],
            new_pos[None, :] <= query_index[:, None],
        )
        visible = visible & (row_index < start + count)[None, :]
        scores = (
            jnp.einsum("qkgd,rkd->kgqr", heads_q, keys_block, preferred_element_type=jnp.float32)
            * scale
        )
        scores = jnp.where(visible[None, None], scores, NEG)
        top_new = jnp.maximum(top, jnp.max(scores, -1))
        weights = jnp.where(visible[None, None], jnp.exp(scores - top_new[..., None]), 0.0)
        shrink = jnp.exp(top - top_new)
        total = total * shrink + jnp.sum(weights, -1)
        summed = summed * shrink[..., None] + jnp.einsum(
            "kgqr,rkd->kgqd",
            weights.astype(jnp.bfloat16),
            values_block,
            preferred_element_type=jnp.float32,
        )
        return ((top_new, total, summed), None)

    state, unused = lax.scan(step_block, carry, (keys_padded, values_padded, block_start))
    return state


def local(
    queries,
    new_keys,
    new_values,
    cache_keys,
    cache_values,
    cache_length,
    residual,
    out_weight,
    norm_gain,
    route_ids,
    route_gates,
    w_gate,
    w_up,
    w_down,
):
    tok_rows = queries.shape[0]
    cache_rows = cache_keys.shape[0]
    ctx_index = lax.axis_index("ctx")
    exp_index = lax.axis_index("exp")
    cache_limit = cache_length[0]
    local_keys = jnp.concatenate([cache_keys, new_keys], 0)
    local_values = jnp.concatenate([cache_values, new_values], 0)
    kv_local = cache_keys.shape[1] // HD
    group = queries.shape[1] // cache_keys.shape[1]
    heads_local = kv_local * group
    initial = (
        jnp.full((kv_local, group, tok_rows), NEG, jnp.float32),
        jnp.zeros((kv_local, group, tok_rows), jnp.float32),
        jnp.zeros((kv_local, group, tok_rows, HD), jnp.float32),
    )
    query_index = ctx_index * tok_rows + jnp.arange(tok_rows, dtype=jnp.int32)
    top, total, summed = attend_piece(
        initial,
        queries,
        query_index,
        lax.all_gather(local_keys, "ctx", axis=0, tiled=True),
        lax.all_gather(local_values, "ctx", axis=0, tiled=True),
        jnp.int32(0),
        cache_rows,
        tok_rows,
        cache_limit,
    )
    attended = (
        (summed / total[..., None])
        .transpose(2, 0, 1, 3)
        .reshape(tok_rows, heads_local * HD)
        .astype(jnp.bfloat16)
    )
    projected = jnp.dot(attended, out_weight, preferred_element_type=jnp.float32)
    sub_rows = residual.shape[0]
    own_first = exp_index * sub_rows
    placed = lax.dynamic_update_slice_in_dim(
        jnp.zeros_like(projected), residual.astype(jnp.float32), own_first, 0
    )
    mixed = lax.psum((projected + placed).astype(jnp.bfloat16), "exp").astype(jnp.float32)
    mean_square = jnp.mean(mixed * mixed, -1, keepdims=True)
    normed = (mixed * lax.rsqrt(mean_square + EPS) * norm_gain.astype(jnp.float32)).astype(
        jnp.bfloat16
    )
    capacity = 3 * tok_rows // lax.axis_size("exp")
    hits = route_ids == exp_index
    row_hit = jnp.any(hits, 1)
    slot = jnp.cumsum(row_hit.astype(jnp.int32)) - 1
    select = (
        (slot[None, :] == jnp.arange(capacity, dtype=jnp.int32)[:, None]) & row_hit[None, :]
    ).astype(jnp.bfloat16)
    outgoing = jnp.dot(select, normed, preferred_element_type=jnp.float32).astype(jnp.bfloat16)
    gate_local = w_gate[0]
    up_local = w_up[0]
    down_local = w_down[0]
    piece = lax.all_gather(outgoing, "ctx", axis=0, tiled=True)
    gate_part = jnp.dot(piece, gate_local, preferred_element_type=jnp.float32)
    up_part = jnp.dot(piece, up_local, preferred_element_type=jnp.float32)
    hidden = (jax.nn.silu(gate_part) * up_part).astype(jnp.bfloat16)
    terms = jnp.dot(hidden, down_local, preferred_element_type=jnp.float32)
    expert_out = lax.psum_scatter(
        terms.astype(jnp.bfloat16), "ctx", scatter_dimension=0, tiled=True
    )
    returned = jnp.dot(jnp.transpose(select), expert_out, preferred_element_type=jnp.float32)
    weight_row = jnp.sum(jnp.where(hits, route_gates, 0.0), 1)
    weighted = weight_row[:, None] * returned
    combined = lax.psum_scatter(
        weighted.astype(jnp.bfloat16), "exp", scatter_dimension=0, tiled=True
    ).astype(jnp.float32)
    own_mixed = lax.dynamic_slice_in_dim(mixed, own_first, sub_rows, 0)
    return (own_mixed + combined).astype(jnp.bfloat16)


def solution(mesh):
    placed = (
        P("ctx", "exp"),
        P("ctx", "exp"),
        P("ctx", "exp"),
        P("ctx", "exp"),
        P("ctx", "exp"),
        P(),
        P(("ctx", "exp"), None),
        P("exp", None),
        P(),
        P("ctx", None),
        P("ctx", None),
        P("exp", None, "ctx"),
        P("exp", None, "ctx"),
        P("exp", "ctx", None),
    )
    return jax.shard_map(
        local, mesh=mesh, in_specs=placed, out_specs=P(("ctx", "exp"), None), check_vma=False
    )
```

profile of v0, /device:TPU:0, one launch (start us, length us, event | category | flops | bytes accessed | tf_op | source)
XLA Modules:
  0.0 558.8 jit_solution(15143822286957495030)
XLA Ops:
  6.5 1.7 pad_maximum_fusion
  8.3 1.7 pad_maximum_fusion.1
  11.3 38.8 %all-gather.4.cloned.1.call-done = bf16[18432,128]{1,0:T(8,128)(2,1)} async-done(((bf16[1152,128]{1,0:T(8,128)(2,1)}), bf16[18432,128]{1,0:T(8,128)(2,1)}) %all-gather.4.cloned.1.call-update) | async-done | bytes 4718608 | tf_op jit(solution)/shard_map/all_gather | solution.py:110
  50.1 40.3 %all-gather.6.cloned.1.call-done = bf16[18432,128]{1,0:T(8,128)(2,1)} async-done(((bf16[1152,128]{1,0:T(8,128)(2,1)}), bf16[18432,128]{1,0:T(8,128)(2,1)}) %all-gather.6.cloned.1.call-update) | async-done | bytes 4718608 | tf_op jit(solution)/shard_map/all_gather | solution.py:111
  90.5 143.8 %while.17 = (s32[]{:T(128)}, f32[1,4,128]{2,1,0:T(4,128)S(1)}, f32[1,4,128]{2,1,0:T(4,128)S(1)}, f32[1,4,128,128]{3,2,1,0:T(8,128)S(1)}, s32[18]{0:T(128)S(1)}, ...) while((s32[]{:T(128)}, f32[1,4,128]{2,1,0:T(4,128)S(1)}, ...), condition=%wide.region_3.4_spmd.clone, body=%wide.region_0.3_spmd.clone.sunk | while | flops 275886208 | bytes 8044705 | solution.py:70
  96.1 1.8 fusion.77
  102.7 1.4 fusion.74
  104.1 1.8 fusion.77
  110.7 1.4 fusion.74
  112.1 1.8 fusion.77
  118.7 1.4 fusion.74
  120.1 1.8 fusion.77
  126.7 1.4 fusion.74
  128.1 1.8 fusion.77
  134.6 1.4 fusion.74
  136.1 1.8 fusion.77
  142.6 1.4 fusion.74
  144.1 1.8 fusion.77
  150.6 1.4 fusion.74
  152.1 1.8 fusion.77
  158.6 1.4 fusion.74
  160.0 1.8 fusion.77
  166.6 1.4 fusion.74
  168.0 1.8 fusion.77
  174.6 1.4 fusion.74
  176.0 1.8 fusion.77
  182.6 1.4 fusion.74
  184.0 1.8 fusion.77
  190.6 1.4 fusion.74
  192.0 1.8 fusion.77
  198.6 1.4 fusion.74
  200.0 1.8 fusion.77
  206.6 1.4 fusion.74
  208.0 1.8 fusion.77
  216.0 1.8 fusion.77
  224.0 1.8 fusion.77
  232.0 1.8 fusion.77
  234.5 3.0 fusion.58
  239.2 87.5 %all-reduce.2.cloned.1.call-done = bf16[128,4096]{1,0:T(8,128)(2,1)} async-done(((bf16[128,4096]{1,0:T(8,128)(2,1)}), bf16[128,4096]{1,0:T(8,128)(2,1)}) %all-reduce.2.cloned.1.call-update) | async-done | bytes 1048592 | tf_op jit(solution)/shard_map/psum | solution.py:129
  326.7 1.5 multiply_reduce_fusion
  328.2 2.5 convolution_convert_fusion
  330.8 40.3 %all-gather.8.cloned.1.call-done = bf16[768,4096]{1,0:T(8,128)(2,1)} async-done(((bf16[48,4096]{1,0:T(8,128)(2,1)}), bf16[768,4096]{1,0:T(8,128)(2,1)}) %all-gather.8.cloned.1.call-update) | async-done | bytes 6291472 | tf_op jit(solution)/shard_map/all_gather | solution.py:145
  371.1 11.9 %fusion.34 = f32[768,896]{1,0:T(8,128)} fusion(bf16[768,4096]{1,0:T(8,128)(2,1)} %all-gather.8.cloned.1.call-done, bf16[1,4096,896]{2,1,0:T(8,128)(2,1)} %param.28), kind=kOutput, calls=%fused_computation.48 | convolution fusion | flops 5637144576 | bytes 16384000 | tf_op jit(solution)/shard_map/dot_general | solution.py:147
  383.1 21.6 %fusion.38 = bf16[768,4096]{1,0:T(8,128)(2,1)} fusion(bf16[1,896,4096]{2,1,0:T(8,128)(2,1)} %param.29, f32[768,896]{1,0:T(8,128)} %fusion.34, bf16[768,4096]{1,0:T(8,128)(2,1)} %all-gather.8.cloned.1.call-done, bf16[1,4096,896]{2,1,0:T(8,128)(2,1)} %param.27), kind=kOutput, calls=%fused_computation.52 | convolution fusion | flops 11281563648 | bytes 30015488 | tf_op jit(solution)/shard_map/dot_general | solution.py:149
  405.4 71.2 %reduce-scatter.3.cloned.1.call-done = bf16[48,4096]{1,0:T(8,128)(2,1)} async-done(((bf16[768,4096]{1,0:T(8,128)(2,1)}), bf16[48,4096]{1,0:T(8,128)(2,1)}) %reduce-scatter.3.cloned.1.call-update) | async-done | bytes 393232 | tf_op jit(solution)/shard_map/reduce_scatter | solution.py:150
  476.6 2.5 fusion.41
  479.3 71.1 %reduce-scatter.5.cloned.1.call-done = bf16[16,4096]{1,0:T(8,128)(2,1)} async-done(((bf16[128,4096]{1,0:T(8,128)(2,1)}), bf16[16,4096]{1,0:T(8,128)(2,1)}) %reduce-scatter.5.cloned.1.call-update) | async-done | bytes 131088 | tf_op jit(solution)/shard_map/reduce_scatter | solution.py:156
  550.4 1.6 add_convert_fusion
  (225 shorter events, 95.4 us)
Async XLA Ops:
  6.5 43.6 %all-gather.4.cloned.1.call-start = ((), (), s32[]{:S(2)}) async-start(), calls=%async_computation.2 | async-start | bytes 5013504 | tf_op jit(solution)/shard_map/all_gather | solution.py:110
  8.3 82.2 %all-gather.6.cloned.1.call-start = ((), (), s32[]{:S(2)}) async-start(), calls=%async_computation.3 | async-start | bytes 5013504 | tf_op jit(solution)/shard_map/all_gather | solution.py:111
  10.0 316.7 %all-reduce.2.cloned.1.call-start = ((), (), s32[]{:S(2)}) async-start(), calls=%async_computation.4 | async-start | bytes 2097152 | tf_op jit(solution)/shard_map/psum | solution.py:129
  234.5 3.0 copy-start.1
  237.5 1.3 copy-start.3
  237.5 1.6 copy-start.2
  238.7 132.5 %all-gather.8.cloned.1.call-start = ((), (), s32[]{:S(2)}) async-start(), calls=%async_computation.5 | async-start | bytes 6684672 | tf_op jit(solution)/shard_map/all_gather | solution.py:145
  330.8 145.8 %reduce-scatter.3.cloned.1.call-start = ((), (), s32[]{:S(2)}) async-start(), calls=%async_computation.6 | async-start | bytes 6684672 | tf_op jit(solution)/shard_map/reduce_scatter | solution.py:150
  404.7 0.7 copy-start.4
  404.8 74.3 %copy-start = (bf16[128,4096]{1,0:T(8,128)(2,1)S(1)}, bf16[128,4096]{1,0:T(8,128)(2,1)}, u32[]{:S(2)}) copy-start(bf16[128,4096]{1,0:T(8,128)(2,1)} %all-reduce.2.cloned.1.call-done) | copy-start | bytes 3145732
  404.8 145.6 %reduce-scatter.5.cloned.1.call-start = ((), (), s32[]{:S(2)}) async-start(), calls=%async_computation.7 | async-start | bytes 1179648 | tf_op jit(solution)/shard_map/reduce_scatter | solution.py:156
Sparse Core Ops, SparseCore 0:
  9.1 41.0 all-gather.3
  51.8 38.5 all-gather.5
  238.8 87.8 all-reduce.1
  330.9 40.2 all-gather.7
  404.9 71.6 reduce-scatter.2
  480.0 70.3 reduce-scatter.4
where the time goes:
time: 561 us; the launch traced here: 559 us
  waiting for transfers between devices  349 us (62%)
  matrix products  98.3 us (18%)
  other arithmetic  82.5 us (15%)
  between operations  13.6 us (2%)
  local copies, waits for them, and re-layouts  13.5 us (2%)
    psum x1, waiting for transfers between devices, local(): lax.psum((projected + placed).astype(jnp.bfloat16), 'exp')  87.5 us
    reduce_scatter x1, waiting for transfers between devices, local(): lax.psum_scatter(terms.astype(jnp.bfloat16), 'ctx', scatter_dimension=0,...  71.2 us
    reduce_scatter x1, waiting for transfers between devices, local(): lax.psum_scatter(weighted.astype(jnp.bfloat16), 'exp', scatter_dimension=...  71.1 us
    all_gather x1, waiting for transfers between devices, local(): lax.all_gather(local_values, 'ctx', axis=0, tiled=True)  40.3 us
    all_gather x1, waiting for transfers between devices, local(): piece = lax.all_gather(outgoing, 'ctx', axis=0, tiled=True)  40.3 us
    all_gather x1, waiting for transfers between devices, local(): lax.all_gather(local_keys, 'ctx', axis=0, tiled=True)  38.8 us
    dot_general x18, matrix products, step_block(): jnp.einsum('kgqr,rkd->kgqd', weights.astype(jnp.bfloat16), values_block,...  31.6 us
    dot_general x18, matrix products, step_block(): jnp.einsum('qkgd,rkd->kgqr', heads_q, keys_block, preferred_element_type=...  25.2 us
  transfers between devices with their start and end apart: 6, of which 6 were waited for; matrix products, arithmetic and copies ran while one was open for 1% of the time, Pallas kernels for 0%

commit v1 on v0

--- a/solution.py
+++ b/solution.py
@@ -134,7 +134,9 @@
     capacity = 3 * tok_rows // lax.axis_size("exp")
     hits = route_ids == exp_index
     row_hit = jnp.any(hits, 1)
-    slot = jnp.cumsum(row_hit.astype(jnp.int32)) - 1
+    order = jnp.arange(tok_rows, dtype=jnp.int32)
+    earlier = row_hit[None, :] & (order[None, :] <= order[:, None])
+    slot = jnp.sum(earlier.astype(jnp.int32), 1) - 1
     select = (
         (slot[None, :] == jnp.arange(capacity, dtype=jnp.int32)[:, None]) & row_hit[None, :]
     ).astype(jnp.bfloat16)

time: 561 us -> 564 us (level)
  no operation moved by 1% of the time
where the time goes in v1:
time: 564 us; the launch traced here: 562 us
  waiting for transfers between devices  350 us (62%)
  matrix products  98.4 us (17%)
  other arithmetic  85 us (15%)
  local copies, waits for them, and re-layouts  13.8 us (2%)
  between operations  13.6 us (2%)
    psum x1, waiting for transfers between devices, local(): lax.psum((projected + placed).astype(jnp.bfloat16), 'exp')  87.8 us
    reduce_scatter x1, waiting for transfers between devices, local(): lax.psum_scatter(terms.astype(jnp.bfloat16), 'ctx', scatter_dimension=0,...  71.1 us
    reduce_scatter x1, waiting for transfers between devices, local(): lax.psum_scatter(weighted.astype(jnp.bfloat16), 'exp', scatter_dimension=...  71 us
    all_gather x1, waiting for transfers between devices, local(): lax.all_gather(local_values, 'ctx', axis=0, tiled=True)  40.3 us
    all_gather x1, waiting for transfers between devices, local(): piece = lax.all_gather(outgoing, 'ctx', axis=0, tiled=True)  40.3 us
    all_gather x1, waiting for transfers between devices, local(): lax.all_gather(local_keys, 'ctx', axis=0, tiled=True)  38.8 us
    dot_general x18, matrix products, step_block(): jnp.einsum('kgqr,rkd->kgqd', weights.astype(jnp.bfloat16), values_block,...  31.6 us
    dot_general x18, matrix products, step_block(): jnp.einsum('qkgd,rkd->kgqr', heads_q, keys_block, preferred_element_type=...  25.2 us
  transfers between devices with their start and end apart: 6, of which 6 were waited for; matrix products, arithmetic and copies ran while one was open for 1% of the time, Pallas kernels for 0%

profile of v1, /device:TPU:0, one launch (start us, length us, event | category | flops | bytes accessed | tf_op | source)
XLA Modules:
  0.0 561.8 jit_solution(11914320667182745474)
XLA Ops:
  6.5 1.7 pad_maximum_fusion
  8.3 1.7 pad_maximum_fusion.1
  11.3 38.8 %all-gather.4.cloned.1.call-done = bf16[18432,128]{1,0:T(8,128)(2,1)} async-done(((bf16[1152,128]{1,0:T(8,128)(2,1)}), bf16[18432,128]{1,0:T(8,128)(2,1)}) %all-gather.4.cloned.1.call-update) | async-done | bytes 4718608 | tf_op jit(solution)/shard_map/all_gather | solution.py:110
  50.1 40.3 %all-gather.6.cloned.1.call-done = bf16[18432,128]{1,0:T(8,128)(2,1)} async-done(((bf16[1152,128]{1,0:T(8,128)(2,1)}), bf16[18432,128]{1,0:T(8,128)(2,1)}) %all-gather.6.cloned.1.call-update) | async-done | bytes 4718608 | tf_op jit(solution)/shard_map/all_gather | solution.py:111
  90.5 146.9 %while.17 = (s32[]{:T(128)}, f32[1,4,128]{2,1,0:T(4,128)S(1)}, f32[1,4,128]{2,1,0:T(4,128)S(1)}, f32[1,4,128,128]{3,2,1,0:T(8,128)S(1)}, s32[18]{0:T(128)S(1)}, ...) while((s32[]{:T(128)}, f32[1,4,128]{2,1,0:T(4,128)S(1)}, ...), condition=%wide.region_3.4_spmd.clone, body=%wide.region_0.3_spmd.clone.sunk | while | flops 275886208 | bytes 8044705 | solution.py:70
  96.3 1.8 fusion.78
  103.0 1.4 fusion.75
  104.4 1.8 fusion.78
  111.2 1.4 fusion.75
  112.6 1.8 fusion.78
  119.3 1.4 fusion.75
  120.8 1.8 fusion.78
  127.5 1.4 fusion.75
  128.9 1.8 fusion.78
  135.7 1.4 fusion.75
  137.1 1.8 fusion.78
  143.8 1.4 fusion.75
  145.2 1.8 fusion.78
  152.0 1.4 fusion.75
  153.4 1.8 fusion.78
  160.1 1.4 fusion.75
  161.6 1.8 fusion.78
  168.3 1.4 fusion.75
  169.7 1.8 fusion.78
  176.5 1.4 fusion.75
  177.9 1.8 fusion.78
  184.6 1.4 fusion.75
  186.0 1.8 fusion.78
  192.8 1.4 fusion.75
  194.2 1.8 fusion.78
  200.9 1.4 fusion.75
  202.4 1.8 fusion.78
  209.1 1.4 fusion.75
  210.5 1.8 fusion.78
  218.7 1.8 fusion.78
  226.8 1.8 fusion.78
  235.0 1.8 fusion.78
  237.5 3.0 fusion.59
  241.9 87.8 %all-reduce.2.cloned.1.call-done = bf16[128,4096]{1,0:T(8,128)(2,1)} async-done(((bf16[128,4096]{1,0:T(8,128)(2,1)}), bf16[128,4096]{1,0:T(8,128)(2,1)}) %all-reduce.2.cloned.1.call-update) | async-done | bytes 1048592 | tf_op jit(solution)/shard_map/psum | solution.py:129
  329.8 1.5 multiply_reduce_fusion
  331.3 2.5 convolution_convert_fusion
  333.8 40.3 %all-gather.8.cloned.1.call-done = bf16[768,4096]{1,0:T(8,128)(2,1)} async-done(((bf16[48,4096]{1,0:T(8,128)(2,1)}), bf16[768,4096]{1,0:T(8,128)(2,1)}) %all-gather.8.cloned.1.call-update) | async-done | bytes 6291472 | tf_op jit(solution)/shard_map/all_gather | solution.py:147
  374.2 12.0 %fusion.34 = f32[768,896]{1,0:T(8,128)} fusion(bf16[768,4096]{1,0:T(8,128)(2,1)} %all-gather.8.cloned.1.call-done, bf16[1,4096,896]{2,1,0:T(8,128)(2,1)} %param.28), kind=kOutput, calls=%fused_computation.48 | convolution fusion | flops 5637144576 | bytes 16384000 | tf_op jit(solution)/shard_map/dot_general | solution.py:149
  386.1 21.7 %fusion.38 = bf16[768,4096]{1,0:T(8,128)(2,1)} fusion(bf16[1,896,4096]{2,1,0:T(8,128)(2,1)} %param.29, f32[768,896]{1,0:T(8,128)} %fusion.34, bf16[768,4096]{1,0:T(8,128)(2,1)} %all-gather.8.cloned.1.call-done, bf16[1,4096,896]{2,1,0:T(8,128)(2,1)} %param.27), kind=kOutput, calls=%fused_computation.52 | convolution fusion | flops 11281563648 | bytes 30015488 | tf_op jit(solution)/shard_map/dot_general | solution.py:151
  408.5 71.1 %reduce-scatter.3.cloned.1.call-done = bf16[48,4096]{1,0:T(8,128)(2,1)} async-done(((bf16[768,4096]{1,0:T(8,128)(2,1)}), bf16[48,4096]{1,0:T(8,128)(2,1)}) %reduce-scatter.3.cloned.1.call-update) | async-done | bytes 393232 | tf_op jit(solution)/shard_map/reduce_scatter | solution.py:152
  479.6 2.5 fusion.41
  482.3 71.0 %reduce-scatter.5.cloned.1.call-done = bf16[16,4096]{1,0:T(8,128)(2,1)} async-done(((bf16[128,4096]{1,0:T(8,128)(2,1)}), bf16[16,4096]{1,0:T(8,128)(2,1)}) %reduce-scatter.5.cloned.1.call-update) | async-done | bytes 131088 | tf_op jit(solution)/shard_map/reduce_scatter | solution.py:158
  553.4 1.6 add_convert_fusion
  (223 shorter events, 98.2 us)
Async XLA Ops:
  6.5 43.6 %all-gather.4.cloned.1.call-start = ((), (), s32[]{:S(2)}) async-start(), calls=%async_computation.2 | async-start | bytes 5013504 | tf_op jit(solution)/shard_map/all_gather | solution.py:110
  8.3 82.2 %all-gather.6.cloned.1.call-start = ((), (), s32[]{:S(2)}) async-start(), calls=%async_computation.3 | async-start | bytes 5013504 | tf_op jit(solution)/shard_map/all_gather | solution.py:111
  10.0 319.7 %all-reduce.2.cloned.1.call-start = ((), (), s32[]{:S(2)}) async-start(), calls=%async_computation.4 | async-start | bytes 2097152 | tf_op jit(solution)/shard_map/psum | solution.py:129
  237.5 3.0 copy-start.1
  240.5 1.3 copy-start.2
  240.5 1.3 copy-start.3
  241.7 132.4 %all-gather.8.cloned.1.call-start = ((), (), s32[]{:S(2)}) async-start(), calls=%async_computation.5 | async-start | bytes 6684672 | tf_op jit(solution)/shard_map/all_gather | solution.py:147
  333.8 145.8 %reduce-scatter.3.cloned.1.call-start = ((), (), s32[]{:S(2)}) async-start(), calls=%async_computation.6 | async-start | bytes 6684672 | tf_op jit(solution)/shard_map/reduce_scatter | solution.py:152
  407.8 0.7 copy-start.4
  407.8 74.3 %copy-start = (bf16[128,4096]{1,0:T(8,128)(2,1)S(1)}, bf16[128,4096]{1,0:T(8,128)(2,1)}, u32[]{:S(2)}) copy-start(bf16[128,4096]{1,0:T(8,128)(2,1)} %all-reduce.2.cloned.1.call-done) | copy-start | bytes 3145732
  407.8 145.5 %reduce-scatter.5.cloned.1.call-start = ((), (), s32[]{:S(2)}) async-start(), calls=%async_computation.7 | async-start | bytes 1179648 | tf_op jit(solution)/shard_map/reduce_scatter | solution.py:158
Sparse Core Ops, SparseCore 0:
  9.1 41.0 all-gather.3
  51.8 38.5 all-gather.5
  241.8 87.8 all-reduce.1
  333.9 40.2 all-gather.7
  407.9 71.6 reduce-scatter.2
  483.1 70.2 reduce-scatter.4

commit v2 on v1

v2 whole, which is shorter than its diff:
```python
import functools
import math

import jax
import jax.numpy as jnp
from jax import lax
from jax.experimental import pallas as pl
from jax.experimental.pallas import tpu as pltpu
from jax.sharding import PartitionSpec as P

HD = 128
NEG = -1e30
EPS = 1e-05
MESH = pl.DeviceIdType.MESH
F32 = jnp.float32
BF16 = jnp.bfloat16


def remote(src, dst, send, recv, where):
    return pltpu.make_async_remote_copy(
        src_ref=src,
        dst_ref=dst,
        send_sem=send,
        recv_sem=recv,
        device_id=where,
        device_id_type=MESH,
    )


def attend_kernel(
    n_ctx,
    n_exp,
    limit_ref,
    q_ref,
    nk_ref,
    nv_ref,
    ck_ref,
    cv_ref,
    res_ref,
    ow_ref,
    gain_ref,
    sel_ref,
    out_ref,
    mixed_ref,
    kbuf,
    vbuf,
    kt,
    vext,
    qbuf,
    osend,
    orecv,
    ssend,
    srecv,
    att,
    ow_v,
    psend,
    precv,
    nbuf,
    kv_send,
    kv_recv,
    q_send,
    q_recv,
    o_send,
    o_recv,
    s_send,
    s_recv,
    p_send,
    p_recv,
    n_send,
    n_recv,
    ow_sem,
):
    n_chip = n_ctx // 2
    me = lax.axis_index("ctx")
    ex = lax.axis_index("exp")
    chip = me // 2
    core = me % 2
    sib = me + 1 - 2 * core
    tok = q_ref.shape[0]
    group = q_ref.shape[1] // HD
    cache = ck_ref.shape[0]
    width = res_ref.shape[1]
    sub = res_ref.shape[0]
    c_all = 2 * cache
    rows = c_all + 2 * tok

    ow_copy = pltpu.make_async_copy(ow_ref, ow_v, ow_sem)
    ow_copy.start()

    barrier = pltpu.get_barrier_semaphore()

    def greet_chip(s, _):
        peer = ((chip + s) % n_chip) * 2 + core
        pl.semaphore_signal(barrier, inc=1, device_id={"ctx": peer}, device_id_type=MESH)
        return 0

    def greet_exp(s, _):
        pl.semaphore_signal(
            barrier, inc=1, device_id={"exp": (ex + s) % n_exp}, device_id_type=MESH
        )
        return 0

    pl.semaphore_signal(barrier, inc=1, device_id={"ctx": sib}, device_id_type=MESH)
    lax.fori_loop(1, n_chip, greet_chip, 0)
    lax.fori_loop(1, n_exp, greet_exp, 0)

    for g in range(group):
        qbuf[chip, g * tok : (g + 1) * tok, :] = q_ref[:, g * HD : (g + 1) * HD]
    kbuf[0:cache, :] = ck_ref[...]
    kbuf[c_all : c_all + tok, :] = nk_ref[...]
    vbuf[0:cache, :] = cv_ref[...]
    vbuf[c_all : c_all + tok, :] = nv_ref[...]

    pl.semaphore_wait(barrier, n_chip + n_exp - 1)

    kv_copies = [
        remote(src, dst, kv_send.at[i], kv_recv.at[i], {"ctx": sib})
        for i, (src, dst) in enumerate(
            [
                (ck_ref, kbuf.at[pl.ds(cache, cache)]),
                (nk_ref, kbuf.at[pl.ds(c_all + tok, tok)]),
                (cv_ref, vbuf.at[pl.ds(cache, cache)]),
                (nv_ref, vbuf.at[pl.ds(c_all + tok, tok)]),
            ]
        )
    ]
    for copy in kv_copies:
        copy.start()

    def q_copy(s):
        peer = ((chip + n_chip - s) % n_chip) * 2 + core
        return remote(
            qbuf.at[chip], qbuf.at[chip], q_send.at[s], q_recv.at[chip], {"ctx": peer}
        )

    def q_start(s, _):
        q_copy(s).start()
        return 0

    lax.fori_loop(1, n_chip, q_start, 0)

    for copy in kv_copies:
        copy.wait_recv()
    kt[...] = kbuf[...].T
    vext[:, 0:HD] = vbuf[...]
    vext[:, HD : 2 * HD] = jnp.ones((rows, HD), BF16)

    limit = limit_ref[0]
    position = lax.broadcasted_iota(jnp.int32, (1, cache), 1)
    bias_own = jnp.where(position + me * cache < limit, 0.0, NEG)
    bias_sib = jnp.where(position + sib * cache < limit, 0.0, NEG)
    cache_bias = jnp.concatenate([bias_own, bias_sib], axis=1)
    t_row = lax.broadcasted_iota(jnp.int32, (tok, 2 * tok), 0)
    t_col = lax.broadcasted_iota(jnp.int32, (tok, 2 * tok), 1)
    lane = lax.broadcasted_iota(jnp.int32, (tok, HD), 1)
    key_at = jnp.where(t_col < tok, t_col + me * tok, t_col - tok + sib * tok)
    scale = math.log2(math.e) / math.sqrt(HD)

    def o_copy(s, src):
        peer = src * 2 + core
        return (
            remote(osend.at[s], orecv.at[chip], o_send.at[s], o_recv.at[chip], {"ctx": peer}),
            remote(ssend.at[s], srecv.at[chip], s_send.at[s], s_recv.at[chip], {"ctx": peer}),
        )

    def step(s, _):
        src = (chip + s) % n_chip

        @pl.when(s > 0)
        def _():
            remote(
                qbuf.at[src], qbuf.at[src], q_send.at[s], q_recv.at[src], {"ctx": src * 2 + core}
            ).wait_recv()

        query_at = t_row + (src * 2 + core) * tok
        new_bias = jnp.where(key_at <= query_at, 0.0, NEG)
        stat = jnp.zeros((tok, HD), F32)
        for g in range(group):
            q = qbuf[src, g * tok : (g + 1) * tok, :]
            sc = jnp.dot(q, kt[:, 0:c_all], preferred_element_type=F32) * scale + cache_bias
            sn = jnp.dot(q, kt[:, c_all:rows], preferred_element_type=F32) * scale + new_bias
            top = jnp.maximum(
                jnp.max(sc, axis=1, keepdims=True), jnp.max(sn, axis=1, keepdims=True)
            )
            pc = jnp.exp2(sc - top).astype(BF16)
            pn = jnp.exp2(sn - top).astype(BF16)
            o = jnp.dot(pc, vext[0:c_all, :], preferred_element_type=F32) + jnp.dot(
                pn, vext[c_all:rows, :], preferred_element_type=F32
            )
            total = o[:, HD : 2 * HD]
            osend[s, g * tok : (g + 1) * tok, :] = (o[:, 0:HD] / total).astype(BF16)
            stat = jnp.where(lane == g, top + jnp.log2(total), stat)
        ssend[s] = stat.T[0:8, :]

        @pl.when(s > 0)
        def _():
            for copy in o_copy(s, src):
                copy.start()

        return 0

    lax.fori_loop(0, n_chip, step, 0)
    orecv[chip] = osend[0]
    srecv[chip] = ssend[0]

    def o_wait(s, _):
        src = (chip + s) % n_chip
        remote(
            osend.at[s], orecv.at[src], o_send.at[s], o_recv.at[src], {"ctx": src * 2 + core}
        ).wait_recv()
        remote(
            ssend.at[s], srecv.at[src], s_send.at[s], s_recv.at[src], {"ctx": src * 2 + core}
        ).wait_recv()
        return 0

    lax.fori_loop(1, n_chip, o_wait, 0)

    stats = srecv[...]
    peak = jnp.max(stats, axis=0, keepdims=True)
    share = jnp.exp2(stats - peak)
    share = share / jnp.sum(share, axis=0, keepdims=True)
    share = share.reshape(n_chip * 8, tok)
    if n_chip * 8 < HD:
        share = jnp.concatenate([share, jnp.zeros((HD - n_chip * 8, tok), F32)], axis=0)
    share = share.T
    for g in range(group):
        value = jnp.zeros((tok, HD), F32)
        for i in range(n_chip):
            part = orecv[i, g * tok : (g + 1) * tok, :].astype(F32)
            value = value + share[:, i * 8 + g : i * 8 + g + 1] * part
        att[:, g * HD : (g + 1) * HD] = value.astype(BF16)

    ow_copy.wait()
    half = width // 2
    tile = min(512, half)

    def p_copy(h, s):
        peer = (ex + s) % n_exp
        columns = pl.ds(h * half, half)
        return remote(
            psend.at[pl.ds(pl.multiple_of(peer * sub, sub), sub), columns],
            precv.at[ex, :, columns],
            p_send.at[h, s],
            p_recv.at[h, ex],
            {"exp": peer},
        )

    for h in range(2):

        def project(n, _, h=h):
            columns = pl.ds(pl.multiple_of(h * half + n * tile, tile), tile)
            psend[:, columns] = jnp.dot(
                att[...], ow_v[:, columns], preferred_element_type=F32
            ).astype(BF16)
            return 0

        lax.fori_loop(0, half // tile, project, 0)

        def p_start(s, _, h=h):
            p_copy(h, s).start()
            return 0

        lax.fori_loop(1, n_exp, p_start, 0)

    precv[ex] = psend[pl.ds(pl.multiple_of(ex * sub, sub), sub), :]
    for h in range(2):
        columns = pl.ds(h * half, half)

        def p_wait(s, _, h=h, columns=columns):
            src = (ex + s) % n_exp
            remote(
                psend.at[pl.ds(0, sub), columns],
                precv.at[src, :, columns],
                p_send.at[h, s],
                p_recv.at[h, src],
                {"exp": src},
            ).wait_recv()
            return 0

        lax.fori_loop(1, n_exp, p_wait, 0)
        value = res_ref[:, columns].astype(F32)
        for j in range(n_exp):
            value = value + precv[j, :, columns].astype(F32)
        mixed_ref[:, columns] = value

    mixed = mixed_ref[...]
    square = jnp.mean(mixed * mixed, axis=1, keepdims=True)
    own = pl.ds(pl.multiple_of(ex * sub, sub), sub)
    nbuf[own, :] = (mixed * lax.rsqrt(square + EPS) * gain_ref[...].astype(F32)).astype(BF16)

    def n_copy(s, row_of, peer):
        at = pl.ds(pl.multiple_of(row_of * sub, sub), sub)
        return remote(nbuf.at[at], nbuf.at[at], n_send.at[s], n_recv.at[row_of], {"exp": peer})

    def n_start(s, _):
        n_copy(s, ex, (ex + s) % n_exp).start()
        return 0

    lax.fori_loop(1, n_exp, n_start, 0)

    def n_wait(s, _):
        src = (ex + s) % n_exp
        n_copy(s, src, src).wait_recv()
        return 0

    lax.fori_loop(1, n_exp, n_wait, 0)
    out_ref[...] = jnp.dot(sel_ref[...], nbuf[...], preferred_element_type=F32).astype(BF16)

    for copy in kv_copies:
        copy.wait_send()

    def drain_chip(s, _):
        q_copy(s).wait_send()
        for copy in o_copy(s, (chip + s) % n_chip):
            copy.wait_send()
        return 0

    def drain_exp(s, _):
        n_copy(s, ex, (ex + s) % n_exp).wait_send()
        for h in range(2):
            p_copy(h, s).wait_send()
        return 0

    lax.fori_loop(1, n_chip, drain_chip, 0)
    lax.fori_loop(1, n_exp, drain_exp, 0)


def attend(limit, q, nk, nv, ck, cv, res, ow, gain, sel):
    n_ctx, n_exp = lax.axis_size("ctx"), lax.axis_size("exp")
    n_chip = n_ctx // 2
    tok, q_width = q.shape
    cache = ck.shape[0]
    sub, width = res.shape
    rows = 2 * (cache + tok)
    block = (q_width // HD) * tok
    vmem = pl.BlockSpec(memory_space=pltpu.VMEM)
    dma = pltpu.SemaphoreType.DMA
    flops = 4 * n_chip * block * rows * HD + 2 * tok * q_width * width
    return pl.pallas_call(
        functools.partial(attend_kernel, n_ctx, n_exp),
        out_shape=(
            jax.ShapeDtypeStruct((sel.shape[0], width), BF16),
            jax.ShapeDtypeStruct((sub, width), F32),
        ),
        in_specs=[pl.BlockSpec(memory_space=pltpu.SMEM)]
        + [vmem] * 6
        + [pl.BlockSpec(memory_space=pl.ANY)]
        + [vmem] * 2,
        out_specs=(vmem, vmem),
        scratch_shapes=[
            pltpu.VMEM((rows, HD), BF16),
            pltpu.VMEM((rows, HD), BF16),
            pltpu.VMEM((HD, rows), BF16),
            pltpu.VMEM((rows, 2 * HD), BF16),
            pltpu.VMEM((n_chip, block, HD), BF16),
            pltpu.VMEM((n_chip, block, HD), BF16),
            pltpu.VMEM((n_chip, block, HD), BF16),
            pltpu.VMEM((n_chip, 8, tok), F32),
            pltpu.VMEM((n_chip, 8, tok), F32),
            pltpu.VMEM((tok, q_width), BF16),
            pltpu.VMEM((q_width, width), BF16),
            pltpu.VMEM((tok, width), BF16),
            pltpu.VMEM((n_exp, sub, width), BF16),
            pltpu.VMEM((tok, width), BF16),
            dma((4,)),
            dma((4,)),
            dma((n_chip,)),
            dma((n_chip,)),
            dma((n_chip,)),
            dma((n_chip,)),
            dma((n_chip,)),
            dma((n_chip,)),
            dma((2, n_exp)),
            dma((2, n_exp)),
            dma((n_exp,)),
            dma((n_exp,)),
            dma,
        ],
        compiler_params=pltpu.CompilerParams(
            collective_id=0, has_side_effects=True, vmem_limit_bytes=48 * 2**20
        ),
        cost_estimate=pl.CostEstimate(
            flops=flops, bytes_accessed=8 * 2**20, transcendentals=n_chip * block * rows
        ),
    )(limit, q, nk, nv, ck, cv, res, ow, gain, sel)


def local(
    queries,
    new_keys,
    new_values,
    cache_keys,
    cache_values,
    cache_length,
    residual,
    out_weight,
    norm_gain,
    route_ids,
    route_gates,
    w_gate,
    w_up,
    w_down,
):
    tok_rows = queries.shape[0]
    exp_index = lax.axis_index("exp")
    capacity = 3 * tok_rows // lax.axis_size("exp")
    hits = route_ids == exp_index
    row_hit = jnp.any(hits, 1)
    order = jnp.arange(tok_rows, dtype=jnp.int32)
    earlier = row_hit[None, :] & (order[None, :] <= order[:, None])
    slot = jnp.sum(earlier.astype(jnp.int32), 1) - 1
    select = (
        (slot[None, :] == jnp.arange(capacity, dtype=jnp.int32)[:, None]) & row_hit[None, :]
    ).astype(BF16)
    outgoing, own_mixed = attend(
        cache_length,
        queries,
        new_keys,
        new_values,
        cache_keys,
        cache_values,
        residual,
        out_weight,
        norm_gain[None, :],
        select,
    )
    piece = lax.all_gather(outgoing, "ctx", axis=0, tiled=True)
    gate_part = jnp.dot(piece, w_gate[0], preferred_element_type=F32)
    up_part = jnp.dot(piece, w_up[0], preferred_element_type=F32)
    hidden = (jax.nn.silu(gate_part) * up_part).astype(BF16)
    terms = jnp.dot(hidden, w_down[0], preferred_element_type=F32)
    expert_out = lax.psum_scatter(terms.astype(BF16), "ctx", scatter_dimension=0, tiled=True)
    returned = jnp.dot(jnp.transpose(select), expert_out, preferred_element_type=F32)
    weight_row = jnp.sum(jnp.where(hits, route_gates, 0.0), 1)
    weighted = weight_row[:, None] * returned
    combined = lax.psum_scatter(
        weighted.astype(BF16), "exp", scatter_dimension=0, tiled=True
    ).astype(F32)
    return (own_mixed + combined).astype(BF16)


def solution(mesh):
    placed = (
        P("ctx", "exp"),
        P("ctx", "exp"),
        P("ctx", "exp"),
        P("ctx", "exp"),
        P("ctx", "exp"),
        P(),
        P(("ctx", "exp"), None),
        P("exp", None),
        P(),
        P("ctx", None),
        P("ctx", None),
        P("exp", None, "ctx"),
        P("exp", None, "ctx"),
        P("exp", "ctx", None),
    )
    return jax.shard_map(
        local, mesh=mesh, in_specs=placed, out_specs=P(("ctx", "exp"), None), check_vma=False
    )
```

time: 564 us -> 316 us (0.56)
  waiting for transfers between devices: 350 us -> 186 us
  other arithmetic: 85 us -> 2.42 us
  Pallas kernels: 0 us -> 70.8 us
  matrix products: 98.4 us -> 33.6 us
    psum x1 -> x0, waiting for transfers between devices: 87.8 us -> none  [local(): lax.psum((projected + placed).astype(jnp.bfloat16), 'exp')]
    all_gather x2 -> x0, waiting for transfers between devices: 79.2 us -> none  [the longest x1 40.3 us: local(): lax.all_gather(local_values, 'ctx', axis=0, tiled=True)]
    pallas_call x0 -> x1, Pallas kernels: none -> 70.8 us  [attend(): pl.pallas_call(functools.partial(attend_kernel, n_ctx, n_exp), out_shape=...]
    dot_general x41 -> x3, matrix products: 98.4 us -> 33.6 us  [the longest x1 21.3 us: local(): terms = jnp.dot(hidden, w_down[0], preferred_element_type=F32)]
    lt x36 -> x0, other arithmetic: 36.5 us -> none  [the longest x18 24.1 us: step_block(): cache_pos < cache_limit]
    and x18 -> x0, other arithmetic: 17.8 us -> none  [step_block(): visible = visible & (row_index < start + count)[None, :]]
    sub x18 -> x0, other arithmetic: 12.4 us -> none  [step_block(): new_pos = shard * new_rows + offset - cache_rows]
    dynamic_slice x18 -> x0, local copies, waits for them, and re-layouts: 11.8 us -> none  [attend_piece(): lax.scan(step_block, carry, (keys_padded, values_padded, block_start))]
  transfers between devices with their start and end apart: 6 -> 3, of which waited for: 6 -> 3; matrix products, arithmetic and copies ran while one was open for 1% -> 0% of each run, Pallas kernels for 0% -> 0%
where the time goes in v2:
time: 316 us; the launch traced here: 315 us
  waiting for transfers between devices  186 us (59%)
  Pallas kernels  70.8 us (22%)
  matrix products  33.6 us (11%)
  between operations  13.8 us (4%)
  local copies, waits for them, and re-layouts  8.73 us (3%)
    reduce_scatter x1, waiting for transfers between devices, local(): lax.psum_scatter(weighted.astype(BF16), 'exp', scatter_dimension=0, tiled...  71.4 us
    reduce_scatter x1, waiting for transfers between devices, local(): lax.psum_scatter(terms.astype(BF16), 'ctx', scatter_dimension=0, tiled=True)  71.1 us
    pallas_call x1, Pallas kernels, attend(): pl.pallas_call(functools.partial(attend_kernel, n_ctx, n_exp), out_shape=...  70.8 us
    all_gather x1, waiting for transfers between devices, local(): piece = lax.all_gather(outgoing, 'ctx', axis=0, tiled=True)  43 us
    dot_general x1, matrix products, local(): terms = jnp.dot(hidden, w_down[0], preferred_element_type=F32)  21.3 us
    dot_general x1, matrix products, local(): up_part = jnp.dot(piece, w_up[0], preferred_element_type=F32)  9.86 us
    unnamed x18, local copies, waits for them, and re-layouts  8.02 us
  transfers between devices with their start and end apart: 3, of which 3 were waited for; matrix products, arithmetic and copies ran while one was open for 0% of the time, Pallas kernels for 0%

profile of v2, /device:TPU:0, one launch (start us, length us, event | category | flops | bytes accessed | tf_op | source)
XLA Modules:
  0.0 315.1 jit_solution(682312789621987707)
XLA Ops:
  6.5 0.0 all-gather.2.cloned.1.call-start
  7.2 0.7 fusion.21
  7.9 0.1 convert_reduce_fusion
  8.0 0.7 broadcast_in_dim.5.gain_ref
  8.7 0.0 copy-start
  8.8 2.2 copy-done
  10.9 0.0 copy-start.1
  10.9 0.9 copy-done.1
  11.9 0.0 copy-start.2
  11.9 0.9 copy-done.2
  12.8 0.0 copy-start.3
  12.8 0.9 copy-done.3
  13.7 0.0 copy-start.4
  13.7 0.9 copy-done.4
  14.6 0.0 copy-start.5
  14.6 0.8 copy-done.5
  15.4 0.0 copy-start.6
  15.4 0.8 copy-done.6
  16.2 70.8 %shard_map.136 = (bf16[48,4096]{1,0:T(8,128)(2,1)}, f32[16,4096]{1,0:T(8,128)S(1)}) custom-call(s32[1]{0:T(128)S(6)} %copy.15.limit_ref, bf16[128,512]{1,0:T(8,128)(2,1)S(1)} %copy-done.3, bf16[128,128]{1,0:T(8,128)(2,1)S(1)} %copy-done.5, bf16[128,128]{1,0:T(8,128)(2,1)S(1)} %copy-done.6, bf16[1024,128]{1,0:T(8,128)(2,1)S(1)} %copy-done.1, ...), custom_call_target="tpu_custom_call" | custom-call | flops 5368709120 | bytes 8388608 | tf_op jit(solution)/shard_map/pallas_call | solution.py:339
  87.0 0.0 all-gather.2.cloned.1.call-update
  87.0 0.0 reduce-scatter.3.cloned.1.call-start
  87.1 43.0 %all-gather.2.cloned.1.call-done = bf16[768,4096]{1,0:T(8,128)(2,1)} async-done(((bf16[48,4096]{1,0:T(8,128)(2,1)}), bf16[768,4096]{1,0:T(8,128)(2,1)}) %all-gather.2.cloned.1.call-update) | async-done | bytes 6291472 | tf_op jit(solution)/shard_map/all_gather | solution.py:427
  130.1 9.9 %fusion.2 = f32[768,896]{1,0:T(8,128)S(1)} fusion(bf16[768,4096]{1,0:T(8,128)(2,1)} %all-gather.2.cloned.1.call-done, bf16[1,4096,896]{2,1,0:T(8,128)(2,1)} %param.26), kind=kOutput, calls=%fused_computation.2 | convolution fusion | flops 5637144576 | bytes 16384000 | tf_op jit(solution)/shard_map/dot_general | solution.py:429
  139.9 21.3 %fusion.6 = bf16[768,4096]{1,0:T(8,128)(2,1)} fusion(bf16[1,896,4096]{2,1,0:T(8,128)(2,1)} %param.27, f32[768,896]{1,0:T(8,128)S(1)} %fusion.2, bf16[768,4096]{1,0:T(8,128)(2,1)} %all-gather.2.cloned.1.call-done, bf16[1,4096,896]{2,1,0:T(8,128)(2,1)} %param.25), kind=kOutput, calls=%fused_computation.6 | convolution fusion | flops 11281563648 | bytes 30015488 | tf_op jit(solution)/shard_map/dot_general | solution.py:431
  161.2 0.0 copy-start.7
  161.3 0.0 copy-start.8
  161.3 0.0 reduce-scatter.3.cloned.1.call-update
  161.3 0.0 reduce-scatter.5.cloned.1.call-start
  161.3 0.6 copy-done.7
  161.9 0.0 copy-done.8
  162.0 71.1 %reduce-scatter.3.cloned.1.call-done = bf16[48,4096]{1,0:T(8,128)(2,1)} async-done(((bf16[768,4096]{1,0:T(8,128)(2,1)}), bf16[48,4096]{1,0:T(8,128)(2,1)}) %reduce-scatter.3.cloned.1.call-update) | async-done | bytes 393232 | tf_op jit(solution)/shard_map/reduce_scatter | solution.py:432
  233.1 2.4 fusion.9
  235.5 0.0 reduce-scatter.5.cloned.1.call-update
  235.6 71.4 %reduce-scatter.5.cloned.1.call-done = bf16[16,4096]{1,0:T(8,128)(2,1)} async-done(((bf16[128,4096]{1,0:T(8,128)(2,1)}), bf16[16,4096]{1,0:T(8,128)(2,1)}) %reduce-scatter.5.cloned.1.call-update) | async-done | bytes 131088 | tf_op jit(solution)/shard_map/reduce_scatter | solution.py:436
  307.0 1.6 add_convert_fusion
  (3 shorter events, 0.0 us)
Async XLA Ops:
  6.5 123.5 %all-gather.2.cloned.1.call-start = ((), (), s32[]{:S(2)}) async-start(), calls=%async_computation.2 | async-start | bytes 6684672 | tf_op jit(solution)/shard_map/all_gather | solution.py:427
  8.7 2.2 copy-start
  10.9 0.9 copy-start.1
  11.9 0.9 copy-start.2
  12.8 0.9 copy-start.3
  13.7 0.9 copy-start.4
  14.6 0.8 copy-start.5
  15.4 0.8 copy-start.6
  87.0 146.1 %reduce-scatter.3.cloned.1.call-start = ((), (), s32[]{:S(2)}) async-start(), calls=%async_computation.3 | async-start | bytes 6684672 | tf_op jit(solution)/shard_map/reduce_scatter | solution.py:432
  161.2 0.7 copy-start.7
  161.3 0.7 copy-start.8
  161.3 145.7 %reduce-scatter.5.cloned.1.call-start = ((), (), s32[]{:S(2)}) async-start(), calls=%async_computation.4 | async-start | bytes 1179648 | tf_op jit(solution)/shard_map/reduce_scatter | solution.py:436
Sparse Core Ops, SparseCore 0:
  87.1 42.8 all-gather.1
  161.4 71.6 reduce-scatter.2
  236.7 70.2 reduce-scatter.4

commit v3 on v2

--- a/solution.py
+++ b/solution.py
@@ -385,6 +385,356 @@
     )(limit, q, nk, nv, ck, cv, res, ow, gain, sel)
 
 
+def expert_kernel(
+    n_ctx,
+    n_exp,
+    chunks,
+    in_ref,
+    wg_ref,
+    wu_ref,
+    wd_ref,
+    back_ref,
+    gate_ref,
+    mixed_ref,
+    out_ref,
+    xall,
+    wg_v,
+    wu_v,
+    wd_v,
+    acc_g,
+    acc_u,
+    hid,
+    tbuf,
+    sbuf,
+    red,
+    hbuf,
+    pbuf,
+    xbuf,
+    wsend,
+    wrecv,
+    wg_sem,
+    wu_sem,
+    wd_sem,
+    a_send,
+    a_recv,
+    r_send,
+    r_recv,
+    e_send,
+    e_recv,
+):
+    n_y = n_ctx // 4
+    me = lax.axis_index("ctx")
+    ex = lax.axis_index("exp")
+    core = me % 2
+    x = me // (2 * n_y)
+    y = (me // 2) % n_y
+    y_up, y_down, y_far = (y + 1) % n_y, (y + n_y - 1) % n_y, (y + 2) % n_y
+    sib = {"ctx": me + 1 - 2 * core}
+    across = {"ctx": ((1 - x) * n_y + y) * 2 + core}
+    up = {"ctx": (x * n_y + y_up) * 2 + core}
+    down = {"ctx": (x * n_y + y_down) * 2 + core}
+    cap, width = in_ref.shape
+    sub = out_ref.shape[0]
+    pair = 2 * cap
+    side = n_y * pair
+    span = width // chunks
+
+    def cols(c):
+        return pl.ds(pl.multiple_of(c * span, span), span)
+
+    def w_copies(c):
+        at = pl.ds(pl.multiple_of(c * span, span), span)
+        return (
+            pltpu.make_async_copy(wg_ref.at[at], wg_v.at[at], wg_sem.at[c]),
+            pltpu.make_async_copy(wu_ref.at[at], wu_v.at[at], wu_sem.at[c]),
+        )
+
+    def w_start(c, _):
+        for copy in w_copies(c):
+            copy.start()
+        return 0
+
+    lax.fori_loop(0, chunks, w_start, 0)
+    wd_copy = pltpu.make_async_copy(wd_ref, wd_v, wd_sem)
+    wd_copy.start()
+
+    barrier = pltpu.get_barrier_semaphore()
+    for where in (sib, across, up, down):
+        pl.semaphore_signal(barrier, inc=1, device_id=where, device_id_type=MESH)
+
+    def greet_exp(s, _):
+        pl.semaphore_signal(
+            barrier, inc=1, device_id={"exp": (ex + s) % n_exp}, device_id_type=MESH
+        )
+        return 0
+
+    lax.fori_loop(1, n_exp, greet_exp, 0)
+
+    def row(k, at, offset=0):
+        return pl.multiple_of(k * side + at * pair + offset, 16)
+
+    own_row = row(core, y, x * cap)
+    xall[pl.ds(own_row, cap), :] = in_ref[...]
+    acc_g[...] = jnp.zeros_like(acc_g)
+    acc_u[...] = jnp.zeros_like(acc_u)
+    pl.semaphore_wait(barrier, 3 + n_exp)
+
+    def gather(kind, c, first, count, where):
+        ref = xall.at[pl.ds(first, count), cols(c)]
+        return remote(ref, ref, a_send.at[kind, c], a_recv.at[kind, c], where)
+
+    def a_x(c):
+        return gather(0, c, own_row, cap, across)
+
+    def a_pairs(c):
+        return (
+            gather(1, c, row(core, y), pair, up),
+            gather(2, c, row(core, y), pair, down),
+            gather(5, c, row(core, y), pair, sib),
+        )
+
+    def a_relays(c):
+        return (
+            gather(3, c, row(core, y_down), cap, up),
+            gather(4, c, row(core, y_up, cap), cap, down),
+            gather(6, c, row(core, y_down), pair, sib),
+            gather(7, c, row(core, y_up), pair, sib),
+        )
+
+    def a_far(c):
+        return gather(8, c, row(core, y_far), pair, sib)
+
+    def a_x_start(c, _):
+        a_x(c).start()
+        return 0
+
+    lax.fori_loop(0, chunks, a_x_start, 0)
+
+    def gather_step(it, _):
+        @pl.when(it < chunks)
+        def _():
+            c = it
+            gather(0, c, row(core, y, (1 - x) * cap), cap, across).wait_recv()
+            for copy in a_pairs(c):
+                copy.start()
+
+        @pl.when((it >= 1) & (it < chunks + 1))
+        def _():
+            c = it - 1
+            gather(1, c, row(core, y_down), pair, down).wait_recv()
+            gather(2, c, row(core, y_up), pair, up).wait_recv()
+            for copy in a_relays(c):
+                copy.start()
+
+        @pl.when((it >= 2) & (it < chunks + 2))
+        def _():
+            c = it - 2
+            gather(3, c, row(core, y_far), cap, down).wait_recv()
+            gather(4, c, row(core, y_far, cap), cap, up).wait_recv()
+            a_far(c).start()
+
+        @pl.when(it >= 3)
+        def _():
+            c = it - 3
+            gather(5, c, row(1 - core, y), pair, sib).wait_recv()
+            gather(6, c, row(1 - core, y_down), pair, sib).wait_recv()
+            gather(7, c, row(1 - core, y_up), pair, sib).wait_recv()
+            gather(8, c, row(1 - core, y_far), pair, sib).wait_recv()
+            for copy in w_copies(c):
+                copy.wait()
+            lhs = xall[:, cols(c)]
+            acc_g[...] += jnp.dot(lhs, wg_v[cols(c), :], preferred_element_type=F32)
+            acc_u[...] += jnp.dot(lhs, wu_v[cols(c), :], preferred_element_type=F32)
+
+        return 0
+
+    lax.fori_loop(0, chunks + 3, gather_step, 0)
+
+    gate = acc_g[...]
+    hid[...] = (gate / (1.0 + jnp.exp(-gate)) * acc_u[...]).astype(BF16)
+    wd_copy.wait()
+
+    def reduce(kind, c, src, dst, where):
+        return remote(src, dst, r_send.at[kind, c], r_recv.at[kind, c], where)
+
+    def r_sib(c):
+        other = pl.ds(pl.multiple_of((1 - core) * side, 16), side)
+        return reduce(0, c, tbuf.at[c, other], sbuf.at[c], sib)
+
+    def block(at, offset, count):
+        return pl.ds(pl.multiple_of(at * pair + offset, 16), count)
+
+    def r_halves(c):
+        return (
+            reduce(1, c, red.at[c, block(y_far, 0, cap)], hbuf.at[0, c], up),
+            reduce(2, c, red.at[c, block(y_far, cap, cap)], hbuf.at[1, c], down),
+        )
+
+    def r_pairs(c):
+        return (
+            reduce(3, c, red.at[c, block(y_up, 0, pair)], pbuf.at[0, c], up),
+            reduce(4, c, red.at[c, block(y_down, 0, pair)], pbuf.at[1, c], down),
+        )
+
+    def r_x(c):
+        return reduce(5, c, red.at[c, block(y, (1 - x) * cap, cap)], xbuf.at[c], across)
+
+    def e_copy(c, s, row_of, slot, peer):
+        at = pl.ds(pl.multiple_of(row_of * sub, sub), sub)
+        return remote(
+            wsend.at[at, cols(c)],
+            wrecv.at[slot, :, cols(c)],
+            e_send.at[s, c],
+            e_recv.at[slot, c],
+            {"exp": peer},
+        )
+
+    def add(c, at, other):
+        red[c, at, :] = (red[c, at, :].astype(F32) + other.astype(F32)).astype(BF16)
+
+    def reduce_step(it, _):
+        @pl.when(it >= 5)
+        def _():
+            c = it - 5
+
+            def wait(s, _):
+                src = (ex + s) % n_exp
+                e_copy(c, s, src, src, src).wait_recv()
+                return 0
+
+            lax.fori_loop(1, n_exp, wait, 0)
+            value = jnp.zeros((sub, span), F32)
+            for j in range(n_exp):
+                value = value + wrecv[j, :, cols(c)].astype(F32)
+            out_ref[:, cols(c)] = (mixed_ref[:, cols(c)] + value).astype(BF16)
+
+        @pl.when((it >= 4) & (it < chunks + 4))
+        def _():
+            c = it - 4
+            r_x(c).wait_recv()
+            own = block(y, x * cap, cap)
+            done = (red[c, own, :].astype(F32) + xbuf[c].astype(F32)).astype(BF16)
+            back = jnp.dot(back_ref[...], done, preferred_element_type=F32)
+            wsend[:, cols(c)] = (gate_ref[...] * back).astype(BF16)
+
+            def start(s, _):
+                peer = (ex + s) % n_exp
+                e_copy(c, s, peer, ex, peer).start()
+                return 0
+
+            lax.fori_loop(1, n_exp, start, 0)
+            own_rows = pl.ds(pl.multiple_of(ex * sub, sub), sub)
+            wrecv[ex, :, cols(c)] = wsend[own_rows, cols(c)]
+
+        @pl.when((it >= 3) & (it < chunks + 3))
+        def _():
+            c = it - 3
+            for copy in r_pairs(c):
+                copy.wait_recv()
+            add(c, block(y, 0, pair), pbuf[0, c].astype(F32) + pbuf[1, c].astype(F32))
+            r_x(c).start()
+
+        @pl.when((it >= 2) & (it < chunks + 2))
+        def _():
+            c = it - 2
+            for copy in r_halves(c):
+                copy.wait_recv()
+            add(c, block(y_up, 0, cap), hbuf[0, c])
+            add(c, block(y_down, cap, cap), hbuf[1, c])
+            for copy in r_pairs(c):
+                copy.start()
+
+        @pl.when((it >= 1) & (it < chunks + 1))
+        def _():
+            c = it - 1
+            r_sib(c).wait_recv()
+            own = pl.ds(pl.multiple_of(core * side, 16), side)
+            red[c] = (tbuf[c, own, :].astype(F32) + sbuf[c].astype(F32)).astype(BF16)
+            for copy in r_halves(c):
+                copy.start()
+
+        @pl.when(it < chunks)
+        def _():
+            c = it
+            tbuf[c] = jnp.dot(hid[...], wd_v[:, cols(c)], preferred_element_type=F32).astype(BF16)
+            r_sib(c).start()
+
+        return 0
+
+    lax.fori_loop(0, chunks + 5, reduce_step, 0)
+
+    def drain(c, _):
+        for copy in (a_x(c), *a_pairs(c), *a_relays(c), a_far(c)):
+            copy.wait_send()
+        for copy in (r_sib(c), *r_halves(c), *r_pairs(c), r_x(c)):
+            copy.wait_send()
+
+        def drain_exp(s, _):
+            peer = (ex + s) % n_exp
+            e_copy(c, s, peer, ex, peer).wait_send()
+            return 0
+
+        lax.fori_loop(1, n_exp, drain_exp, 0)
+        return 0
+
+    lax.fori_loop(0, chunks, drain, 0)
+
+
+def experts(rows_in, wg, wu, wd, back, gate, mixed):
+    n_ctx, n_exp = lax.axis_size("ctx"), lax.axis_size("exp")
+    cap, width = rows_in.shape
+    hidden = wg.shape[1]
+    tok = back.shape[0]
+    sub = mixed.shape[0]
+    chunks = 8
+    span = width // chunks
+    total = n_ctx * cap
+    side = total // 2
+    vmem = pl.BlockSpec(memory_space=pltpu.VMEM)
+    hbm = pl.BlockSpec(memory_space=pl.ANY)
+    dma = pltpu.SemaphoreType.DMA
+    return pl.pallas_call(
+        functools.partial(expert_kernel, n_ctx, n_exp, chunks),
+        out_shape=jax.ShapeDtypeStruct((sub, width), BF16),
+        in_specs=[vmem, hbm, hbm, hbm, vmem, vmem, vmem],
+        out_specs=vmem,
+        scratch_shapes=[
+            pltpu.VMEM((total, width), BF16),
+            pltpu.VMEM((width, hidden), BF16),
+            pltpu.VMEM((width, hidden), BF16),
+            pltpu.VMEM((hidden, width), BF16),
+            pltpu.VMEM((total, hidden), F32),
+            pltpu.VMEM((total, hidden), F32),
+            pltpu.VMEM((total, hidden), BF16),
+            pltpu.VMEM((chunks, total, span), BF16),
+            pltpu.VMEM((chunks, side, span), BF16),
+            pltpu.VMEM((chunks, side, span), BF16),
+            pltpu.VMEM((2, chunks, cap, span), BF16),
+            pltpu.VMEM((2, chunks, 2 * cap, span), BF16),
+            pltpu.VMEM((chunks, cap, span), BF16),
+            pltpu.VMEM((tok, width), BF16),
+            pltpu.VMEM((n_exp, sub, width), BF16),
+            dma((chunks,)),
+            dma((chunks,)),
+            dma,
+            dma((9, chunks)),
+            dma((9, chunks)),
+            dma((6, chunks)),
+            dma((6, chunks)),
+            dma((n_exp, chunks)),
+            dma((n_exp, chunks)),
+        ],
+        compiler_params=pltpu.CompilerParams(
+            collective_id=1, has_side_effects=True, vmem_limit_bytes=60 * 2**20
+        ),
+        cost_estimate=pl.CostEstimate(
+            flops=6 * total * width * hidden,
+            bytes_accessed=6 * width * hidden,
+            transcendentals=total * hidden,
+        ),
+    )(rows_in, wg, wu, wd, back, gate, mixed)
+
+
 def local(
     queries,
     new_keys,
@@ -424,19 +774,16 @@
         norm_gain[None, :],
         select,
     )
-    piece = lax.all_gather(outgoing, "ctx", axis=0, tiled=True)
-    gate_part = jnp.dot(piece, w_gate[0], preferred_element_type=F32)
-    up_part = jnp.dot(piece, w_up[0], preferred_element_type=F32)
-    hidden = (jax.nn.silu(gate_part) * up_part).astype(BF16)
-    terms = jnp.dot(hidden, w_down[0], preferred_element_type=F32)
-    expert_out = lax.psum_scatter(terms.astype(BF16), "ctx", scatter_dimension=0, tiled=True)
-    returned = jnp.dot(jnp.transpose(select), expert_out, preferred_element_type=F32)
     weight_row = jnp.sum(jnp.where(hits, route_gates, 0.0), 1)
-    weighted = weight_row[:, None] * returned
-    combined = lax.psum_scatter(
-        weighted.astype(BF16), "exp", scatter_dimension=0, tiled=True
-    ).astype(F32)
-    return (own_mixed + combined).astype(BF16)
+    return experts(
+        outgoing,
+        w_gate[0],
+        w_up[0],
+        w_down[0],
+        jnp.transpose(select),
+        weight_row[:, None],
+        own_mixed,
+    )
 
 
 def solution(mesh):

time: 316 us -> 195 us (0.62)
  waiting for transfers between devices: 186 us -> 0 us
  Pallas kernels: 70.8 us -> 179 us
  matrix products: 33.6 us -> 0 us
  between operations: 13.8 us -> 0.71 us
  local copies, waits for them, and re-layouts: 8.73 us -> 11.9 us
    reduce_scatter x2 -> x0, waiting for transfers between devices: 143 us -> none  [the longest x1 71.4 us: local(): lax.psum_scatter(weighted.astype(BF16), 'exp', scatter_dimension=0, tiled...]
    pallas_call x0 -> x1, Pallas kernels: none -> 109 us  [experts(): pl.pallas_call(functools.partial(expert_kernel, n_ctx, n_exp, chunks), ou...]
    all_gather x1 -> x0, waiting for transfers between devices: 43 us -> none  [local(): piece = lax.all_gather(outgoing, 'ctx', axis=0, tiled=True)]
    dot_general x3 -> x0, matrix products: 33.6 us -> none  [the longest x1 21.3 us: local(): terms = jnp.dot(hidden, w_down[0], preferred_element_type=F32)]
    unnamed x18 -> x19, local copies, waits for them, and re-layouts: 8.02 us -> 10.4 us
  transfers between devices with their start and end apart: 3 -> 0, of which waited for: 3 -> 0; matrix products, arithmetic and copies ran while one was open for 0% -> 0% of each run, Pallas kernels for 0% -> 0%
where the time goes in v3:
time: 195 us; the launch traced here: 194 us
  Pallas kernels  179 us (92%)
  local copies, waits for them, and re-layouts  11.9 us (6%)
  other arithmetic  2.23 us (1%)
    pallas_call x1, Pallas kernels, experts(): pl.pallas_call(functools.partial(expert_kernel, n_ctx, n_exp, chunks), ou...  109 us
    pallas_call x1, Pallas kernels, attend(): pl.pallas_call(functools.partial(attend_kernel, n_ctx, n_exp), out_shape=...  70.1 us
    unnamed x19, local copies, waits for them, and re-layouts  10.4 us

profile of v3, /device:TPU:0, one launch (start us, length us, event | category | flops | bytes accessed | tf_op | source)
XLA Modules:
  0.0 194.0 jit_solution(1798851794158683743)
XLA Ops:
  0.7 0.7 fusion.5
  1.4 0.7 select_reduce_fusion
  2.1 0.1 convert_reduce_fusion
  2.2 0.7 broadcast_in_dim.7.gain_ref
  2.9 0.7 fusion.2.back_ref
  3.6 0.7 copy.16.gate_ref
  4.4 0.0 copy-start
  4.4 2.2 %copy-done = bf16[512,4096]{1,0:T(8,128)(2,1)S(1)} copy-done((bf16[512,4096]{1,0:T(8,128)(2,1)S(1)}, bf16[512,4096]{1,0:T(8,128)(2,1)}, u32[]{:S(2)}) %copy-start) | copy-done | bytes 4194328
  6.5 0.0 copy-start.1
  6.6 0.9 copy-done.1
  7.5 0.0 copy-start.2
  7.5 0.9 copy-done.2
  8.4 0.0 copy-start.3
  8.5 0.9 copy-done.3
  9.4 0.0 copy-start.4
  9.4 0.9 copy-done.4
  10.3 0.0 copy-start.5
  10.3 0.8 copy-done.5
  11.0 0.0 copy-start.6
  11.0 0.8 copy-done.6
  11.8 70.1 %shard_map.136 = (bf16[48,4096]{1,0:T(8,128)(2,1)S(1)}, f32[16,4096]{1,0:T(8,128)S(1)}) custom-call(s32[1]{0:T(128)S(6)} %copy.18.limit_ref, bf16[128,512]{1,0:T(8,128)(2,1)S(1)} %copy-done.3, bf16[128,128]{1,0:T(8,128)(2,1)S(1)} %copy-done.5, bf16[128,128]{1,0:T(8,128)(2,1)S(1)} %copy-done.6, bf16[1024,128]{1,0:T(8,128)(2,1)S(1)} %copy-done.1, ...), custom_call_target="tpu_custom_call" | custom-call | flops 5368709120 | bytes 8388608 | tf_op jit(solution)/shard_map/pallas_call | solution.py:339
  81.8 0.0 copy-start.7
  81.9 0.7 copy-done.7
  82.6 0.0 copy-start.8
  82.6 0.7 copy-done.8
  83.3 109.2 %shard_map.137 = bf16[16,4096]{1,0:T(8,128)(2,1)} custom-call(bf16[48,4096]{1,0:T(8,128)(2,1)} %copy-done.7, bf16[4096,896]{1,0:T(8,128)(2,1)} %bitcast.5, bf16[4096,896]{1,0:T(8,128)(2,1)} %bitcast.6, bf16[896,4096]{1,0:T(8,128)(2,1)} %bitcast.7, bf16[128,48]{1,0:T(8,128)(2,1)} %fusion.2.back_ref, f32[128,1]{1,0:T(8,128)} %copy.16.gate_ref, ...), custom_call_target="tpu_custom_call" | custom-call | flops 16911433728 | bytes 22020096 | tf_op jit(solution)/shard_map/pallas_call | solution.py:696
  192.5 1.6 copy.19
  (2 shorter events, 0.0 us)
Async XLA Ops:
  4.4 2.2 %copy-start = (bf16[512,4096]{1,0:T(8,128)(2,1)S(1)}, bf16[512,4096]{1,0:T(8,128)(2,1)}, u32[]{:S(2)}) copy-start(bf16[512,4096]{1,0:T(8,128)(2,1)} %ow_ref.1) | copy-start | bytes 12582916
  6.5 0.9 copy-start.1
  7.5 0.9 copy-start.2
  8.4 0.9 copy-start.3
  9.4 0.9 copy-start.4
  10.3 0.8 copy-start.5
  11.0 0.8 copy-start.6
  81.8 0.7 copy-start.7
  82.6 0.7 copy-start.8

commit v4 on v2

--- a/solution.py
+++ b/solution.py
@@ -25,6 +25,10 @@
         device_id=where,
         device_id_type=MESH,
     )
+
+
+def arrived(ref, sem):
+    pltpu.make_async_copy(ref, ref, sem).wait()
 
 
 def attend_kernel(
@@ -39,8 +43,7 @@
     res_ref,
     ow_ref,
     gain_ref,
-    sel_ref,
-    out_ref,
+    normed_ref,
     mixed_ref,
     kbuf,
     vbuf,
@@ -55,7 +58,9 @@
     ow_v,
     psend,
     precv,
-    nbuf,
+    res_v,
+    gain_v,
+    in_sem,
     kv_send,
     kv_recv,
     q_send,
@@ -66,8 +71,6 @@
     s_recv,
     p_send,
     p_recv,
-    n_send,
-    n_recv,
     ow_sem,
 ):
     n_chip = n_ctx // 2
@@ -79,14 +82,11 @@
     tok = q_ref.shape[0]
     group = q_ref.shape[1] // HD
     cache = ck_ref.shape[0]
-    width = res_ref.shape[1]
-    sub = res_ref.shape[0]
+    sub, width = res_ref.shape
     c_all = 2 * cache
     rows = c_all + 2 * tok
 
     ow_copy = pltpu.make_async_copy(ow_ref, ow_v, ow_sem)
-    ow_copy.start()
-
     barrier = pltpu.get_barrier_semaphore()
 
     def greet_chip(s, _):
@@ -104,13 +104,22 @@
     lax.fori_loop(1, n_chip, greet_chip, 0)
     lax.fori_loop(1, n_exp, greet_exp, 0)
 
-    for g in range(group):
-        qbuf[chip, g * tok : (g + 1) * tok, :] = q_ref[:, g * HD : (g + 1) * HD]
-    kbuf[0:cache, :] = ck_ref[...]
-    kbuf[c_all : c_all + tok, :] = nk_ref[...]
-    vbuf[0:cache, :] = cv_ref[...]
-    vbuf[c_all : c_all + tok, :] = nv_ref[...]
-
+    moves = [
+        (q_ref.at[:, pl.ds(g * HD, HD)], qbuf.at[chip, pl.ds(g * tok, tok)]) for g in range(group)
+    ]
+    moves += [
+        (ck_ref, kbuf.at[pl.ds(0, cache)]),
+        (nk_ref, kbuf.at[pl.ds(c_all, tok)]),
+        (cv_ref, vbuf.at[pl.ds(0, cache)]),
+        (nv_ref, vbuf.at[pl.ds(c_all, tok)]),
+        (res_ref, res_v),
+        (gain_ref, gain_v),
+    ]
+    loads = [pltpu.make_async_copy(a, b, in_sem.at[i]) for i, (a, b) in enumerate(moves)]
+    for load in loads:
+        load.start()
+    for load in loads[0:group]:
+        load.wait()
     pl.semaphore_wait(barrier, n_chip + n_exp - 1)
 
     kv_copies = [
@@ -130,7 +139,7 @@
     def q_copy(s):
         peer = ((chip + n_chip - s) % n_chip) * 2 + core
         return remote(
-            qbuf.at[chip], qbuf.at[chip], q_send.at[s], q_recv.at[chip], {"ctx": peer}
+            qbuf.at[chip], qbuf.at[chip], q_send, q_recv.at[chip], {"ctx": peer}
         )
 
     def q_start(s, _):
@@ -138,6 +147,9 @@
         return 0
 
     lax.fori_loop(1, n_chip, q_start, 0)
+    ow_copy.start()
+    for load in loads[group:]:
+        load.wait()
 
     for copy in kv_copies:
         copy.wait_recv()
@@ -159,8 +171,8 @@
     def o_copy(s, src):
         peer = src * 2 + core
         return (
-            remote(osend.at[s], orecv.at[chip], o_send.at[s], o_recv.at[chip], {"ctx": peer}),
-            remote(ssend.at[s], srecv.at[chip], s_send.at[s], s_recv.at[chip], {"ctx": peer}),
+            remote(osend.at[s], orecv.at[chip], o_send, o_recv, {"ctx": peer}),
+            remote(ssend.at[s], srecv.at[chip], s_send, s_recv, {"ctx": peer}),
         )
 
     def step(s, _):
@@ -168,9 +180,7 @@
 
         @pl.when(s > 0)
         def _():
-            remote(
-                qbuf.at[src], qbuf.at[src], q_send.at[s], q_recv.at[src], {"ctx": src * 2 + core}
-            ).wait_recv()
+            arrived(qbuf.at[src], q_recv.at[src])
 
         query_at = t_row + (src * 2 + core) * tok
         new_bias = jnp.where(key_at <= query_at, 0.0, NEG)
@@ -203,17 +213,8 @@
     orecv[chip] = osend[0]
     srecv[chip] = ssend[0]
 
-    def o_wait(s, _):
-        src = (chip + s) % n_chip
-        remote(
-            osend.at[s], orecv.at[src], o_send.at[s], o_recv.at[src], {"ctx": src * 2 + core}
-        ).wait_recv()
-        remote(
-            ssend.at[s], srecv.at[src], s_send.at[s], s_recv.at[src], {"ctx": src * 2 + core}
-        ).wait_recv()
-        return 0
-
-    lax.fori_loop(1, n_chip, o_wait, 0)
+    arrived(orecv.at[pl.ds(0, n_chip - 1)], o_recv)
+    arrived(srecv.at[pl.ds(0, n_chip - 1)], s_recv)
 
     stats = srecv[...]
     peak = jnp.max(stats, axis=0, keepdims=True)
@@ -240,8 +241,8 @@
         return remote(
             psend.at[pl.ds(pl.multiple_of(peer * sub, sub), sub), columns],
             precv.at[ex, :, columns],
-            p_send.at[h, s],
-            p_recv.at[h, ex],
+            p_send,
+            p_recv.at[h],
             {"exp": peer},
         )
 
@@ -266,66 +267,26 @@
     for h in range(2):
         columns = pl.ds(h * half, half)
 
-        def p_wait(s, _, h=h, columns=columns):
-            src = (ex + s) % n_exp
-            remote(
-                psend.at[pl.ds(0, sub), columns],
-                precv.at[src, :, columns],
-                p_send.at[h, s],
-                p_recv.at[h, src],
-                {"exp": src},
-            ).wait_recv()
-            return 0
-
-        lax.fori_loop(1, n_exp, p_wait, 0)
-        value = res_ref[:, columns].astype(F32)
+        arrived(psend.at[pl.ds(0, (n_exp - 1) * sub), columns], p_recv.at[h])
+        value = res_v[:, columns].astype(F32)
         for j in range(n_exp):
             value = value + precv[j, :, columns].astype(F32)
         mixed_ref[:, columns] = value
 
     mixed = mixed_ref[...]
     square = jnp.mean(mixed * mixed, axis=1, keepdims=True)
-    own = pl.ds(pl.multiple_of(ex * sub, sub), sub)
-    nbuf[own, :] = (mixed * lax.rsqrt(square + EPS) * gain_ref[...].astype(F32)).astype(BF16)
-
-    def n_copy(s, row_of, peer):
-        at = pl.ds(pl.multiple_of(row_of * sub, sub), sub)
-        return remote(nbuf.at[at], nbuf.at[at], n_send.at[s], n_recv.at[row_of], {"exp": peer})
-
-    def n_start(s, _):
-        n_copy(s, ex, (ex + s) % n_exp).start()
-        return 0
-
-    lax.fori_loop(1, n_exp, n_start, 0)
-
-    def n_wait(s, _):
-        src = (ex + s) % n_exp
-        n_copy(s, src, src).wait_recv()
-        return 0
-
-    lax.fori_loop(1, n_exp, n_wait, 0)
-    out_ref[...] = jnp.dot(sel_ref[...], nbuf[...], preferred_element_type=F32).astype(BF16)
+    normed_ref[...] = (mixed * lax.rsqrt(square + EPS) * gain_v[...].astype(F32)).astype(BF16)
 
     for copy in kv_copies:
         copy.wait_send()
 
-    def drain_chip(s, _):
-        q_copy(s).wait_send()
-        for copy in o_copy(s, (chip + s) % n_chip):
-            copy.wait_send()
-        return 0
-
-    def drain_exp(s, _):
-        n_copy(s, ex, (ex + s) % n_exp).wait_send()
-        for h in range(2):
-            p_copy(h, s).wait_send()
-        return 0
-
-    lax.fori_loop(1, n_chip, drain_chip, 0)
-    lax.fori_loop(1, n_exp, drain_exp, 0)
-
-
-def attend(limit, q, nk, nv, ck, cv, res, ow, gain, sel):
+    arrived(qbuf.at[pl.ds(0, n_chip - 1)], q_send)
+    arrived(osend.at[pl.ds(0, n_chip - 1)], o_send)
+    arrived(ssend.at[pl.ds(0, n_chip - 1)], s_send)
+    arrived(psend.at[pl.ds(0, (n_exp - 1) * sub)], p_send)
+
+
+def attend(limit, q, nk, nv, ck, cv, res, ow, gain):
     n_ctx, n_exp = lax.axis_size("ctx"), lax.axis_size("exp")
     n_chip = n_ctx // 2
     tok, q_width = q.shape
@@ -339,13 +300,11 @@
     return pl.pallas_call(
         functools.partial(attend_kernel, n_ctx, n_exp),
         out_shape=(
-            jax.ShapeDtypeStruct((sel.shape[0], width), BF16),
+            jax.ShapeDtypeStruct((sub, width), BF16),
             jax.ShapeDtypeStruct((sub, width), F32),
         ),
         in_specs=[pl.BlockSpec(memory_space=pltpu.SMEM)]
-        + [vmem] * 6
-        + [pl.BlockSpec(memory_space=pl.ANY)]
-        + [vmem] * 2,
+        + [pl.BlockSpec(memory_space=pl.ANY)] * 8,
         out_specs=(vmem, vmem),
         scratch_shapes=[
             pltpu.VMEM((rows, HD), BF16),
@@ -361,28 +320,480 @@
             pltpu.VMEM((q_width, width), BF16),
             pltpu.VMEM((tok, width), BF16),
             pltpu.VMEM((n_exp, sub, width), BF16),
-            pltpu.VMEM((tok, width), BF16),
+            pltpu.VMEM((sub, width), BF16),
+            pltpu.VMEM((1, width), BF16),
+            dma((q_width // HD + 6,)),
             dma((4,)),
             dma((4,)),
+            dma,
             dma((n_chip,)),
-            dma((n_chip,)),
-            dma((n_chip,)),
-            dma((n_chip,)),
-            dma((n_chip,)),
-            dma((n_chip,)),
-            dma((2, n_exp)),
-            dma((2, n_exp)),
-            dma((n_exp,)),
-            dma((n_exp,)),
+            dma,
+            dma,
+            dma,
+            dma,
+            dma,
+            dma((2,)),
             dma,
         ],
         compiler_params=pltpu.CompilerParams(
-            collective_id=0, has_side_effects=True, vmem_limit_bytes=48 * 2**20
+            collective_id=0, has_side_effects=True, vmem_limit_bytes=60 * 2**20
         ),
         cost_estimate=pl.CostEstimate(
             flops=flops, bytes_accessed=8 * 2**20, transcendentals=n_chip * block * rows
         ),
-    )(limit, q, nk, nv, ck, cv, res, ow, gain, sel)
+    )(limit, q, nk, nv, ck, cv, res, ow, gain)
+
+
+def expert_kernel(
+    n_ctx,
+    n_exp,
+    chunks,
+    cap,
+    normed_ref,
+    wg_ref,
+    wu_ref,
+    wd_ref,
+    ids_ref,
+    gates_ref,
+    mixed_ref,
+    out_ref,
+    nbuf,
+    sel_v,
+    back_v,
+    slot_gate,
+    mixed_v,
+    xall,
+    wg_v,
+    wu_v,
+    wd_v,
+    acc_g,
+    acc_u,
+    hid,
+    tbuf,
+    sbuf,
+    red,
+    ybuf,
+    xbuf,
+    fbuf,
+    wsend,
+    wrecv,
+    wg_sem,
+    wu_sem,
+    wd_sem,
+    in_sem,
+    n_send,
+    n_recv,
+    a_send,
+    a_recv,
+    r_send,
+    r_recv,
+    e_send,
+    e_recv,
+):
+    n_y = n_ctx // 4
+    me = lax.axis_index("ctx")
+    ex = lax.axis_index("exp")
+    k = me % 2
+    x = me // (2 * n_y)
+    y = (me // 2) % n_y
+    y_up, y_down, y_far = (y + 1) % n_y, (y + n_y - 1) % n_y, (y + 2) % n_y
+    sib = {"ctx": me + 1 - 2 * k}
+    across = {"ctx": ((1 - x) * n_y + y) * 2 + k}
+    up = {"ctx": (x * n_y + y_up) * 2 + k}
+    down = {"ctx": (x * n_y + y_down) * 2 + k}
+    far = {"ctx": (x * n_y + y_far) * 2 + k}
+    sub, width = out_ref.shape
+    tok = sub * n_exp
+    total = n_ctx * cap
+    side = total // 2
+    span = width // chunks
+    own_rows = pl.ds(pl.multiple_of(ex * sub, sub), sub)
+
+    def cols(c):
+        return pl.ds(pl.multiple_of(c * span, span), span)
+
+    barrier = pltpu.get_barrier_semaphore()
+    for where in (sib, across, up, down, far):
+        pl.semaphore_signal(barrier, inc=1, device_id=where, device_id_type=MESH)
+
+    def greet_exp(s, _):
+        pl.semaphore_signal(
+            barrier, inc=1, device_id={"exp": (ex + s) % n_exp}, device_id_type=MESH
+        )
+        return 0
+
+    lax.fori_loop(1, n_exp, greet_exp, 0)
+    own_load = pltpu.make_async_copy(normed_ref, nbuf.at[own_rows], in_sem.at[0])
+    own_load.start()
+    pl.semaphore_wait(barrier, 4 + n_exp)
+
+    def n_copy(c, s, row_of, peer):
+        at = pl.ds(pl.multiple_of(row_of * sub, sub), sub)
+        return remote(
+            normed_ref.at[:, cols(c)],
+            nbuf.at[at, cols(c)],
+            n_send,
+            n_recv.at[c],
+            {"exp": peer},
+        )
+
+    def n_start(c, _):
+        def one(s, _):
+            n_copy(c, s, ex, (ex + s) % n_exp).start()
+            return 0
+
+        lax.fori_loop(1, n_exp, one, 0)
+        return 0
+
+    lax.fori_loop(0, chunks, n_start, 0)
+
+    def w_copies(c):
+        at = pl.ds(pl.multiple_of(c * span, span), span)
+        return (
+            pltpu.make_async_copy(wg_ref.at[at], wg_v.at[at], wg_sem.at[c]),
+            pltpu.make_async_copy(wu_ref.at[at], wu_v.at[at], wu_sem.at[c]),
+        )
+
+    def w_start(c, _):
+        for copy in w_copies(c):
+            copy.start()
+        return 0
+
+    lax.fori_loop(0, chunks, w_start, 0)
+    wd_copy = pltpu.make_async_copy(wd_ref, wd_v, wd_sem)
+    wd_copy.start()
+    mixed_copy = pltpu.make_async_copy(mixed_ref, mixed_v, in_sem.at[1])
+    mixed_copy.start()
+
+    slots = -(-cap // HD) * HD
+    first, second = ids_ref[0:1, :] == ex, ids_ref[1:2, :] == ex
+    hit = jnp.where(first, 1.0, 0.0) + jnp.where(second, 1.0, 0.0)
+    weight = jnp.where(first, gates_ref[0:1, :], 0.0) + jnp.where(second, gates_ref[1:2, :], 0.0)
+    earlier = lax.broadcasted_iota(jnp.int32, (tok, tok), 0) <= lax.broadcasted_iota(
+        jnp.int32, (tok, tok), 1
+    )
+    count = jnp.dot(
+        jnp.broadcast_to(hit, (16, tok)).astype(BF16),
+        jnp.where(earlier, 1.0, 0.0).astype(BF16),
+        preferred_element_type=F32,
+    )
+    place = lax.broadcasted_iota(jnp.int32, (slots, tok), 0).astype(F32)
+    chosen = jnp.where(place == count[0:1, :] - 1.0, hit, 0.0)
+    sel_v[...] = chosen[0:cap, :].astype(BF16)
+    back_v[...] = chosen.T[:, 0:cap].astype(BF16)
+    slot_gate[...] = jnp.sum(chosen * weight, axis=1, keepdims=True)[0:cap, :]
+    acc_g[...] = jnp.zeros_like(acc_g)
+    acc_u[...] = jnp.zeros_like(acc_u)
+    own_load.wait()
+
+    half = chunks // 2
+
+    def gather(kind, c, at, where):
+        ref = xall.at[(c, *at)]
+        return remote(ref, ref, a_send.at[kind], a_recv.at[min(kind, 3), c], where)
+
+    def a_own(c):
+        return [gather(0, c, (k, x, y), where) for where in (up, down, far)]
+
+    def a_pass(c):
+        return [gather(1, c, (k, 1 - x, y), where) for where in (up, down, far)]
+
+    def a_block(c):
+        return gather(2, c, (k, x, y), across)
+
+    def a_plane(c):
+        ref = xall.at[c, k, x]
+        return remote(ref, ref, a_send.at[4], a_recv.at[2, c], across)
+
+    def a_sib(c, plane):
+        return gather(3, c, (k, plane), sib)
+
+    three = pl.ds(0, 3)
+
+    def gather_step(it, _):
+        @pl.when(it < chunks)
+        def _():
+            c = it
+
+            arrived(nbuf.at[pl.ds(0, (n_exp - 1) * sub), cols(c)], n_recv.at[c])
+            xall[c, k, x, y] = jnp.dot(
+                sel_v[...], nbuf[:, cols(c)], preferred_element_type=F32
+            ).astype(BF16)
+
+            @pl.when(c % 2 == 0)
+            def _():
+                a_block(c).start()
+
+            for copy in a_own(c):
+                copy.start()
+
+        @pl.when((it >= 2) & (it < chunks + 2))
+        def _():
+            c = it - 2
+
+            @pl.when(c % 2 == 0)
+            def _():
+                arrived(xall.at[c, k, 1 - x, y], a_recv.at[2, c])
+                for copy in a_pass(c):
+                    copy.start()
+                arrived(xall.at[c, k, x, three], a_recv.at[0, c])
+
+            @pl.when(c % 2 == 1)
+            def _():
+                arrived(xall.at[c, k, x, three], a_recv.at[0, c])
+                a_plane(c).start()
+
+            a_sib(c, x).start()
+
+        @pl.when((it >= 4) & (it < chunks + 4))
+        def _():
+            c = it - 4
+
+            @pl.when(c % 2 == 0)
+            def _():
+                arrived(xall.at[c, k, 1 - x, three], a_recv.at[1, c])
+
+            @pl.when(c % 2 == 1)
+            def _():
+                arrived(xall.at[c, k, 1 - x], a_recv.at[2, c])
+
+            a_sib(c, 1 - x).start()
+
+        @pl.when(it >= 5)
+        def _():
+            c = it - 5
+            arrived(xall.at[c, 1 - k], a_recv.at[3, c])
+            for copy in w_copies(c):
+                copy.wait()
+            lhs = xall[c].reshape(total, span)
+            acc_g[...] += jnp.dot(lhs, wg_v[cols(c), :], preferred_element_type=F32)
+            acc_u[...] += jnp.dot(lhs, wu_v[cols(c), :], preferred_element_type=F32)
+
+        return 0
+
+    lax.fori_loop(0, chunks + 5, gather_step, 0)
+
+    gate = acc_g[...]
+    hid[...] = (gate / (1.0 + jnp.exp(-gate)) * acc_u[...]).astype(BF16)
+    wd_copy.wait()
+    mixed_copy.wait()
+
+    def reduce(kind, c, src, dst, where):
+        return remote(src, dst, r_send.at[kind], r_recv.at[kind, c], where)
+
+    def r_sib(c):
+        return reduce(0, c, tbuf.at[c], sbuf.at[c], sib)
+
+    def r_pairs(c):
+        return (
+            reduce(1, c, red.at[c, :, y_up], ybuf.at[c // 2, 0], up),
+            reduce(1, c, red.at[c, :, y_down], ybuf.at[c // 2, 1], down),
+            reduce(1, c, red.at[c, :, y_far], ybuf.at[c // 2, 2], far),
+        )
+
+    def r_block(c):
+        return reduce(2, c, red.at[c, 1 - x, y], fbuf.at[c, 0], across)
+
+    def r_plane(c):
+        return reduce(3, c, red.at[c, 1 - x], xbuf.at[c // 2], across)
+
+    def r_own(c):
+        return (
+            reduce(4, c, red.at[c, x, y_up], fbuf.at[c, 0], up),
+            reduce(4, c, red.at[c, x, y_down], fbuf.at[c, 1], down),
+            reduce(4, c, red.at[c, x, y_far], fbuf.at[c, 2], far),
+        )
+
+    def e_copy(c, s, row_of, slot, peer):
+        at = pl.ds(pl.multiple_of(row_of * sub, sub), sub)
+        return remote(
+            wsend.at[at, cols(c)],
+            wrecv.at[slot, :, cols(c)],
+            e_send,
+            e_recv.at[c],
+            {"exp": peer},
+        )
+
+    other_half = pl.ds(pl.multiple_of((1 - k) * side, 16), side)
+    own_half = pl.ds(pl.multiple_of(k * side, 16), side)
+    shape = (2, n_y, cap, span)
+
+    def reduce_step(it, _):
+        @pl.when(it < chunks)
+        def _():
+            c = it
+            tbuf[c] = (
+                jnp.dot(hid[other_half, :], wd_v[:, cols(c)], preferred_element_type=F32)
+                .astype(BF16)
+                .reshape(shape)
+            )
+            r_sib(c).start()
+            red[c] = (
+                jnp.dot(hid[own_half, :], wd_v[:, cols(c)], preferred_element_type=F32)
+                .astype(BF16)
+                .reshape(shape)
+            )
+
+        @pl.when((it >= 1) & (it < chunks + 1))
+        def _():
+            c = it - 1
+            arrived(sbuf.at[c], r_recv.at[0, c])
+            red[c] = (red[c].astype(F32) + sbuf[c].astype(F32)).astype(BF16)
+
+            @pl.when(c % 2 == 0)
+            def _():
+                for copy in r_pairs(c):
+                    copy.start()
+
+            @pl.when(c % 2 == 1)
+            def _():
+                r_plane(c).start()
+
+        @pl.when((it >= 3) & (it < chunks + 3))
+        def _():
+            c = it - 3
+
+            @pl.when(c % 2 == 0)
+            def _():
+                arrived(ybuf.at[c // 2], r_recv.at[1, c])
+                for px in range(2):
+                    value = red[c, px, y].astype(F32)
+                    for i in range(3):
+                        value = value + ybuf[c // 2, i, px].astype(F32)
+                    red[c, px, y] = value.astype(BF16)
+                r_block(c).start()
+
+            @pl.when(c % 2 == 1)
+            def _():
+                arrived(xbuf.at[c // 2], r_recv.at[3, c])
+                red[c, x] = (red[c, x].astype(F32) + xbuf[c // 2].astype(F32)).astype(BF16)
+                for copy in r_own(c):
+                    copy.start()
+
+        @pl.when((it >= 5) & (it < chunks + 5))
+        def _():
+            c = it - 5
+
+            @pl.when(c % 2 == 0)
+            def _():
+                arrived(fbuf.at[c, 0], r_recv.at[2, c])
+                value = red[c, x, y].astype(F32) + fbuf[c, 0].astype(F32)
+                red[c, x, y] = value.astype(BF16)
+
+            @pl.when(c % 2 == 1)
+            def _():
+                arrived(fbuf.at[c], r_recv.at[4, c])
+                value = red[c, x, y].astype(F32)
+                for i in range(3):
+                    value = value + fbuf[c, i].astype(F32)
+                red[c, x, y] = value.astype(BF16)
+
+            scaled = (slot_gate[...] * red[c, x, y].astype(F32)).astype(BF16)
+            wsend[:, cols(c)] = jnp.dot(
+                back_v[...], scaled, preferred_element_type=F32
+            ).astype(BF16)
+
+            def start(s, _):
+                peer = (ex + s) % n_exp
+                e_copy(c, s, peer, ex, peer).start()
+                return 0
+
+            lax.fori_loop(1, n_exp, start, 0)
+            wrecv[ex, :, cols(c)] = wsend[own_rows, cols(c)]
+
+        @pl.when(it >= 7)
+        def _():
+            c = it - 7
+
+            arrived(wsend.at[pl.ds(0, (n_exp - 1) * sub), cols(c)], e_recv.at[c])
+            value = mixed_v[:, cols(c)]
+            for j in range(n_exp):
+                value = value + wrecv[j, :, cols(c)].astype(F32)
+            out_ref[:, cols(c)] = value.astype(BF16)
+
+        return 0
+
+    lax.fori_loop(0, chunks + 7, reduce_step, 0)
+
+    few = pl.ds(0, half)
+    for i, ref in enumerate(
+        [
+            xall.at[:, 0, 0, three],
+            xall.at[few, 0, 0, three],
+            xall.at[few, 0, 0, 0],
+            xall.at[:, 0],
+            xall.at[few, 0, 0],
+        ]
+    ):
+        arrived(ref, a_send.at[i])
+    for i, ref in enumerate([tbuf, ybuf, fbuf.at[few, 0], xbuf, fbuf.at[few]]):
+        arrived(ref, r_send.at[i])
+    others = pl.ds(0, (n_exp - 1) * sub)
+    arrived(nbuf.at[others], n_send)
+    arrived(wsend.at[others], e_send)
+
+
+def experts(normed, wg, wu, wd, ids, gates, mixed):
+    n_ctx, n_exp = lax.axis_size("ctx"), lax.axis_size("exp")
+    sub, width = normed.shape
+    hidden = wg.shape[1]
+    tok = ids.shape[1]
+    cap = 3 * tok // n_exp
+    chunks = 8
+    span = width // chunks
+    total = n_ctx * cap
+    n_y = n_ctx // 4
+    vmem = pl.BlockSpec(memory_space=pltpu.VMEM)
+    hbm = pl.BlockSpec(memory_space=pl.ANY)
+    dma = pltpu.SemaphoreType.DMA
+    return pl.pallas_call(
+        functools.partial(expert_kernel, n_ctx, n_exp, chunks, cap),
+        out_shape=jax.ShapeDtypeStruct((sub, width), BF16),
+        in_specs=[hbm, hbm, hbm, hbm, vmem, vmem, hbm],
+        out_specs=vmem,
+        scratch_shapes=[
+            pltpu.VMEM((tok, width), BF16),
+            pltpu.VMEM((cap, tok), BF16),
+            pltpu.VMEM((tok, cap), BF16),
+            pltpu.VMEM((cap, 1), F32),
+            pltpu.VMEM((sub, width), F32),
+            pltpu.VMEM((chunks, 2, 2, n_y, cap, span), BF16),
+            pltpu.VMEM((width, hidden), BF16),
+            pltpu.VMEM((width, hidden), BF16),
+            pltpu.VMEM((hidden, width), BF16),
+            pltpu.VMEM((total, hidden), F32),
+            pltpu.VMEM((total, hidden), F32),
+            pltpu.VMEM((total, hidden), BF16),
+            pltpu.VMEM((chunks, 2, n_y, cap, span), BF16),
+            pltpu.VMEM((chunks, 2, n_y, cap, span), BF16),
+            pltpu.VMEM((chunks, 2, n_y, cap, span), BF16),
+            pltpu.VMEM((chunks // 2, 3, 2, cap, span), BF16),
+            pltpu.VMEM((chunks // 2, n_y, cap, span), BF16),
+            pltpu.VMEM((chunks, 3, cap, span), BF16),
+            pltpu.VMEM((tok, width), BF16),
+            pltpu.VMEM((n_exp, sub, width), BF16),
+            dma((chunks,)),
+            dma((chunks,)),
+            dma,
+            dma((2,)),
+            dma,
+            dma((chunks,)),
+            dma((5,)),
+            dma((4, chunks)),
+            dma((5,)),
+            dma((5, chunks)),
+            dma,
+            dma((chunks,)),
+        ],
+        compiler_params=pltpu.CompilerParams(
+            collective_id=1, has_side_effects=True, vmem_limit_bytes=60 * 2**20
+        ),
+        cost_estimate=pl.CostEstimate(
+            flops=6 * total * width * hidden,
+            bytes_accessed=6 * width * hidden,
+            transcendentals=total * hidden,
+        ),
+    )(normed, wg, wu, wd, ids, gates, mixed)
 
 
 def local(
@@ -401,18 +812,7 @@
     w_up,
     w_down,
 ):
-    tok_rows = queries.shape[0]
-    exp_index = lax.axis_index("exp")
-    capacity = 3 * tok_rows // lax.axis_size("exp")
-    hits = route_ids == exp_index
-    row_hit = jnp.any(hits, 1)
-    order = jnp.arange(tok_rows, dtype=jnp.int32)
-    earlier = row_hit[None, :] & (order[None, :] <= order[:, None])
-    slot = jnp.sum(earlier.astype(jnp.int32), 1) - 1
-    select = (
-        (slot[None, :] == jnp.arange(capacity, dtype=jnp.int32)[:, None]) & row_hit[None, :]
-    ).astype(BF16)
-    outgoing, own_mixed = attend(
+    normed, own_mixed = attend(
         cache_length,
         queries,
         new_keys,
@@ -422,21 +822,10 @@
         residual,
         out_weight,
         norm_gain[None, :],
-        select,
     )
-    piece = lax.all_gather(outgoing, "ctx", axis=0, tiled=True)
-    gate_part = jnp.dot(piece, w_gate[0], preferred_element_type=F32)
-    up_part = jnp.dot(piece, w_up[0], preferred_element_type=F32)
-    hidden = (jax.nn.silu(gate_part) * up_part).astype(BF16)
-    terms = jnp.dot(hidden, w_down[0], preferred_element_type=F32)
-    expert_out = lax.psum_scatter(terms.astype(BF16), "ctx", scatter_dimension=0, tiled=True)
-    returned = jnp.dot(jnp.transpose(select), expert_out, preferred_element_type=F32)
-    weight_row = jnp.sum(jnp.where(hits, route_gates, 0.0), 1)
-    weighted = weight_row[:, None] * returned
-    combined = lax.psum_scatter(
-        weighted.astype(BF16), "exp", scatter_dimension=0, tiled=True
-    ).astype(F32)
-    return (own_mixed + combined).astype(BF16)
+    return experts(
+        normed, w_gate[0], w_up[0], w_down[0], route_ids.T, route_gates.T, own_mixed
+    )
 
 
 def solution(mesh):

time: 316 us -> 153 us (0.48)
  waiting for transfers between devices: 186 us -> 0 us
  Pallas kernels: 70.8 us -> 149 us
  matrix products: 33.6 us -> 0 us
  between operations: 13.8 us -> 0.67 us
  local copies, waits for them, and re-layouts: 8.73 us -> 2.88 us
    reduce_scatter x2 -> x0, waiting for transfers between devices: 143 us -> none  [the longest x1 71.4 us: local(): lax.psum_scatter(weighted.astype(BF16), 'exp', scatter_dimension=0, tiled...]
    pallas_call x0 -> x1, Pallas kernels: none -> 92.3 us  [experts(): pl.pallas_call(functools.partial(expert_kernel, n_ctx, n_exp, chunks, cap...]
    all_gather x1 -> x0, waiting for transfers between devices: 43 us -> none  [local(): piece = lax.all_gather(outgoing, 'ctx', axis=0, tiled=True)]
    dot_general x3 -> x0, matrix products: 33.6 us -> none  [the longest x1 21.3 us: local(): terms = jnp.dot(hidden, w_down[0], preferred_element_type=F32)]
    pallas_call x1, Pallas kernels: 70.8 us -> 56.7 us  [attend(): pl.pallas_call(functools.partial(attend_kernel, n_ctx, n_exp), out_shape=...]
    unnamed x18 -> x1, local copies, waits for them, and re-layouts: 8.02 us -> 1.57 us
  transfers between devices with their start and end apart: 3 -> 0, of which waited for: 3 -> 0; matrix products, arithmetic and copies ran while one was open for 0% -> 0% of each run, Pallas kernels for 0% -> 0%
where the time goes in v4:
time: 153 us
  Pallas kernels  149 us (97%)
  local copies, waits for them, and re-layouts  2.88 us (2%)
    pallas_call x1, Pallas kernels, experts(): pl.pallas_call(functools.partial(expert_kernel, n_ctx, n_exp, chunks, cap...  92.3 us
    pallas_call x1, Pallas kernels, attend(): pl.pallas_call(functools.partial(attend_kernel, n_ctx, n_exp), out_shape=...  56.7 us

profile of v4, /device:TPU:0, one launch (start us, length us, event | category | flops | bytes accessed | tf_op | source)
XLA Modules:
  0.0 152.6 jit_solution(3004184167105028007)
XLA Ops:
  0.7 1.3 broadcast_in_dim.3.gain_ref
  2.0 56.7 %shard_map.136 = (bf16[16,4096]{1,0:T(8,128)(2,1)}, f32[16,4096]{1,0:T(8,128)}) custom-call(s32[1]{0:T(128)S(6)} %copy.16.limit_ref, bf16[128,512]{1,0:T(8,128)(2,1)} %q_ref.1, bf16[128,128]{1,0:T(8,128)(2,1)} %nk_ref.1, bf16[128,128]{1,0:T(8,128)(2,1)} %nv_ref.1, bf16[1024,128]{1,0:T(8,128)(2,1)} %ck_ref.1, bf16[1024,128]{1,0:T(8,128)(2,1)} %cv_ref.1, ...), custom_call_target="tpu_custom_call" | custom-call | flops 5368709120 | bytes 8388608 | tf_op jit(solution)/shard_map/pallas_call | solution.py:300
  58.7 92.3 %shard_map.137 = bf16[16,4096]{1,0:T(8,128)(2,1)} custom-call(bf16[16,4096]{1,0:T(8,128)(2,1)} %get-tuple-element.7.normed_ref, bf16[4096,896]{1,0:T(8,128)(2,1)} %bitcast.5, bf16[4096,896]{1,0:T(8,128)(2,1)} %bitcast.6, bf16[896,4096]{1,0:T(8,128)(2,1)} %bitcast.7, s32[2,128]{1,0:T(2,128)} %bitcast.8, f32[2,128]{1,0:T(2,128)} %bitcast.9, ...), custom_call_target="tpu_custom_call" | custom-call | flops 16911433728 | bytes 22020096 | tf_op jit(solution)/shard_map/pallas_call | solution.py:749
  151.1 1.6 %copy.17 = bf16[16,4096]{1,0:T(8,128)(2,1)} copy(bf16[16,4096]{1,0:T(8,128)(2,1)} %shard_map.137) | data formatting | bytes 262144

commit v5 on v4

v5 whole, which is shorter than its diff:
```python
import functools
import math

import jax
import jax.numpy as jnp
from jax import lax
from jax.experimental import pallas as pl
from jax.experimental.pallas import tpu as pltpu
from jax.sharding import PartitionSpec as P

HD = 128
NEG = -1e30
EPS = 1e-05
MESH = pl.DeviceIdType.MESH
F32 = jnp.float32
BF16 = jnp.bfloat16


def remote(src, dst, send, recv, where):
    return pltpu.make_async_remote_copy(
        src_ref=src,
        dst_ref=dst,
        send_sem=send,
        recv_sem=recv,
        device_id=where,
        device_id_type=MESH,
    )


def arrived(ref, sem):
    pltpu.make_async_copy(ref, ref, sem).wait()


def attend_kernel(
    n_ctx,
    n_exp,
    limit_ref,
    q_ref,
    nk_ref,
    nv_ref,
    ck_ref,
    cv_ref,
    res_ref,
    ow_ref,
    gain_ref,
    normed_ref,
    mixed_ref,
    prepare,
    load_weights,
    kbuf,
    vbuf,
    kt,
    vext,
    qbuf,
    osend,
    orecv,
    ssend,
    srecv,
    att,
    ow_v,
    psend,
    precv,
    res_v,
    gain_v,
    in_sem,
    kv_send,
    kv_recv,
    q_send,
    q_recv,
    o_send,
    o_recv,
    s_send,
    s_recv,
    p_send,
    p_recv,
    ow_sem,
):
    n_chip = n_ctx // 2
    me = lax.axis_index("ctx")
    ex = lax.axis_index("exp")
    chip = me // 2
    core = me % 2
    sib = me + 1 - 2 * core
    tok = q_ref.shape[0]
    group = q_ref.shape[1] // HD
    cache = ck_ref.shape[0]
    sub, width = res_ref.shape
    c_all = 2 * cache
    rows = c_all + 2 * tok

    ow_copy = pltpu.make_async_copy(ow_ref, ow_v, ow_sem)
    barrier = pltpu.get_barrier_semaphore()

    def greet_chip(s, _):
        peer = ((chip + s) % n_chip) * 2 + core
        pl.semaphore_signal(barrier, inc=1, device_id={"ctx": peer}, device_id_type=MESH)
        return 0

    def greet_exp(s, _):
        pl.semaphore_signal(
            barrier, inc=1, device_id={"exp": (ex + s) % n_exp}, device_id_type=MESH
        )
        return 0

    pl.semaphore_signal(barrier, inc=1, device_id={"ctx": sib}, device_id_type=MESH)
    lax.fori_loop(1, n_chip, greet_chip, 0)
    lax.fori_loop(1, n_exp, greet_exp, 0)

    moves = [
        (q_ref.at[:, pl.ds(g * HD, HD)], qbuf.at[chip, pl.ds(g * tok, tok)]) for g in range(group)
    ]
    moves += [
        (ck_ref, kbuf.at[pl.ds(0, cache)]),
        (nk_ref, kbuf.at[pl.ds(c_all, tok)]),
        (cv_ref, vbuf.at[pl.ds(0, cache)]),
        (nv_ref, vbuf.at[pl.ds(c_all, tok)]),
        (res_ref, res_v),
        (gain_ref, gain_v),
    ]
    loads = [pltpu.make_async_copy(a, b, in_sem.at[i]) for i, (a, b) in enumerate(moves)]
    for load in loads:
        load.start()
    for load in loads[0:group]:
        load.wait()
    prepare()
    pl.semaphore_wait(barrier, n_chip + n_exp - 1)

    kv_copies = [
        remote(src, dst, kv_send.at[i], kv_recv.at[i], {"ctx": sib})
        for i, (src, dst) in enumerate(
            [
                (ck_ref, kbuf.at[pl.ds(cache, cache)]),
                (nk_ref, kbuf.at[pl.ds(c_all + tok, tok)]),
                (cv_ref, vbuf.at[pl.ds(cache, cache)]),
                (nv_ref, vbuf.at[pl.ds(c_all + tok, tok)]),
            ]
        )
    ]
    for copy in kv_copies:
        copy.start()

    def q_copy(s):
        peer = ((chip + n_chip - s) % n_chip) * 2 + core
        return remote(
            qbuf.at[chip], qbuf.at[chip], q_send, q_recv.at[chip], {"ctx": peer}
        )

    def q_start(s, _):
        q_copy(s).start()
        return 0

    lax.fori_loop(1, n_chip, q_start, 0)
    ow_copy.start()
    load_weights()
    for load in loads[group:]:
        load.wait()

    for copy in kv_copies:
        copy.wait_recv()
    kt[...] = kbuf[...].T
    vext[:, 0:HD] = vbuf[...]
    vext[:, HD : 2 * HD] = jnp.ones((rows, HD), BF16)

    limit = limit_ref[0]
    position = lax.broadcasted_iota(jnp.int32, (1, cache), 1)
    bias_own = jnp.where(position + me * cache < limit, 0.0, NEG)
    bias_sib = jnp.where(position + sib * cache < limit, 0.0, NEG)
    cache_bias = jnp.concatenate([bias_own, bias_sib], axis=1)
    t_row = lax.broadcasted_iota(jnp.int32, (tok, 2 * tok), 0)
    t_col = lax.broadcasted_iota(jnp.int32, (tok, 2 * tok), 1)
    lane = lax.broadcasted_iota(jnp.int32, (tok, HD), 1)
    key_at = jnp.where(t_col < tok, t_col + me * tok, t_col - tok + sib * tok)
    scale = math.log2(math.e) / math.sqrt(HD)

    def o_copy(s, src):
        peer = src * 2 + core
        return (
            remote(osend.at[s], orecv.at[chip], o_send, o_recv, {"ctx": peer}),
            remote(ssend.at[s], srecv.at[chip], s_send, s_recv, {"ctx": peer}),
        )

    def step(s, _):
        src = (chip + s) % n_chip

        @pl.when(s > 0)
        def _():
            arrived(qbuf.at[src], q_recv.at[src])

        query_at = t_row + (src * 2 + core) * tok
        new_bias = jnp.where(key_at <= query_at, 0.0, NEG)
        stat = jnp.zeros((tok, HD), F32)
        for g in range(group):
            q = qbuf[src, g * tok : (g + 1) * tok, :]
            sc = jnp.dot(q, kt[:, 0:c_all], preferred_element_type=F32) * scale + cache_bias
            sn = jnp.dot(q, kt[:, c_all:rows], preferred_element_type=F32) * scale + new_bias
            top = jnp.maximum(
                jnp.max(sc, axis=1, keepdims=True), jnp.max(sn, axis=1, keepdims=True)
            )
            pc = jnp.exp2(sc - top).astype(BF16)
            pn = jnp.exp2(sn - top).astype(BF16)
            o = jnp.dot(pc, vext[0:c_all, :], preferred_element_type=F32) + jnp.dot(
                pn, vext[c_all:rows, :], preferred_element_type=F32
            )
            total = o[:, HD : 2 * HD]
            osend[s, g * tok : (g + 1) * tok, :] = (o[:, 0:HD] / total).astype(BF16)
            stat = jnp.where(lane == g, top + jnp.log2(total), stat)
        ssend[s] = stat.T[0:8, :]

        @pl.when(s > 0)
        def _():
            for copy in o_copy(s, src):
                copy.start()

        return 0

    lax.fori_loop(0, n_chip, step, 0)
    orecv[chip] = osend[0]
    srecv[chip] = ssend[0]

    arrived(orecv.at[pl.ds(0, n_chip - 1)], o_recv)
    arrived(srecv.at[pl.ds(0, n_chip - 1)], s_recv)

    stats = srecv[...]
    peak = jnp.max(stats, axis=0, keepdims=True)
    share = jnp.exp2(stats - peak)
    share = share / jnp.sum(share, axis=0, keepdims=True)
    share = share.reshape(n_chip * 8, tok)
    if n_chip * 8 < HD:
        share = jnp.concatenate([share, jnp.zeros((HD - n_chip * 8, tok), F32)], axis=0)
    share = share.T
    for g in range(group):
        value = jnp.zeros((tok, HD), F32)
        for i in range(n_chip):
            part = orecv[i, g * tok : (g + 1) * tok, :].astype(F32)
            value = value + share[:, i * 8 + g : i * 8 + g + 1] * part
        att[:, g * HD : (g + 1) * HD] = value.astype(BF16)

    ow_copy.wait()
    half = width // 2
    tile = min(512, half)

    def p_copy(h, s):
        peer = (ex + s) % n_exp
        columns = pl.ds(h * half, half)
        return remote(
            psend.at[pl.ds(pl.multiple_of(peer * sub, sub), sub), columns],
            precv.at[ex, :, columns],
            p_send,
            p_recv.at[h],
            {"exp": peer},
        )

    for h in range(2):

        def project(n, _, h=h):
            columns = pl.ds(pl.multiple_of(h * half + n * tile, tile), tile)
            psend[:, columns] = jnp.dot(
                att[...], ow_v[:, columns], preferred_element_type=F32
            ).astype(BF16)
            return 0

        lax.fori_loop(0, half // tile, project, 0)

        def p_start(s, _, h=h):
            p_copy(h, s).start()
            return 0

        lax.fori_loop(1, n_exp, p_start, 0)

    precv[ex] = psend[pl.ds(pl.multiple_of(ex * sub, sub), sub), :]
    for h in range(2):
        columns = pl.ds(h * half, half)

        arrived(psend.at[pl.ds(0, (n_exp - 1) * sub), columns], p_recv.at[h])
        value = res_v[:, columns].astype(F32)
        for j in range(n_exp):
            value = value + precv[j, :, columns].astype(F32)
        mixed_ref[:, columns] = value

    mixed = mixed_ref[...]
    square = jnp.mean(mixed * mixed, axis=1, keepdims=True)
    normed_ref[...] = (mixed * lax.rsqrt(square + EPS) * gain_v[...].astype(F32)).astype(BF16)

    def drain():
        for copy in kv_copies:
            copy.wait_send()
        arrived(qbuf.at[pl.ds(0, n_chip - 1)], q_send)
        arrived(osend.at[pl.ds(0, n_chip - 1)], o_send)
        arrived(ssend.at[pl.ds(0, n_chip - 1)], s_send)
        arrived(psend.at[pl.ds(0, (n_exp - 1) * sub)], p_send)

    return drain


def select_slots(ids_ref, gates_ref, sel_v, back_v, slot_gate):
    ex = lax.axis_index("exp")
    cap, tok = sel_v.shape
    slots = -(-cap // HD) * HD
    first, second = ids_ref[0:1, :] == ex, ids_ref[1:2, :] == ex
    hit = jnp.where(first, 1.0, 0.0) + jnp.where(second, 1.0, 0.0)
    weight = jnp.where(first, gates_ref[0:1, :], 0.0) + jnp.where(second, gates_ref[1:2, :], 0.0)
    earlier = lax.broadcasted_iota(jnp.int32, (tok, tok), 0) <= lax.broadcasted_iota(
        jnp.int32, (tok, tok), 1
    )
    count = jnp.dot(
        jnp.broadcast_to(hit, (16, tok)).astype(BF16),
        jnp.where(earlier, 1.0, 0.0).astype(BF16),
        preferred_element_type=F32,
    )
    place = lax.broadcasted_iota(jnp.int32, (slots, tok), 0).astype(F32)
    chosen = jnp.where(place == count[0:1, :] - 1.0, hit, 0.0)
    sel_v[...] = chosen[0:cap, :].astype(BF16)
    back_v[...] = chosen.T[:, 0:cap].astype(BF16)
    slot_gate[...] = jnp.sum(chosen * weight, axis=1, keepdims=True)[0:cap, :]


def expert_kernel(
    n_ctx,
    n_exp,
    chunks,
    waves,
    cap,
    w_copies,
    wd_copy,
    normed_ref,
    out_ref,
    nbuf,
    sel_v,
    back_v,
    slot_gate,
    mixed_v,
    xall,
    wg_v,
    wu_v,
    wd_v,
    acc_g,
    acc_u,
    hid,
    tbuf,
    sbuf,
    dbuf,
    ybuf,
    xbuf,
    fbuf,
    wsend,
    wrecv,
    n_send,
    n_recv,
    a_send,
    a_recv,
    r_send,
    r_recv,
    e_send,
    e_recv,
):
    n_y = n_ctx // 4
    me = lax.axis_index("ctx")
    ex = lax.axis_index("exp")
    k = me % 2
    x = me // (2 * n_y)
    y = (me // 2) % n_y
    y_up, y_down, y_far = (y + 1) % n_y, (y + n_y - 1) % n_y, (y + 2) % n_y
    sib = {"ctx": me + 1 - 2 * k}
    across = {"ctx": ((1 - x) * n_y + y) * 2 + k}
    up = {"ctx": (x * n_y + y_up) * 2 + k}
    down = {"ctx": (x * n_y + y_down) * 2 + k}
    far = {"ctx": (x * n_y + y_far) * 2 + k}
    sub, width = out_ref.shape
    tok = sub * n_exp
    total = n_ctx * cap
    part = cap // waves
    steps = waves * chunks
    span = width // chunks
    own_rows = pl.ds(pl.multiple_of(ex * sub, sub), sub)

    def cols(c):
        return pl.ds(pl.multiple_of(c * span, span), span)

    nbuf[own_rows, :] = normed_ref[...]

    def n_copy(c, s, row_of, peer):
        at = pl.ds(pl.multiple_of(row_of * sub, sub), sub)
        return remote(
            normed_ref.at[:, cols(c)],
            nbuf.at[at, cols(c)],
            n_send,
            n_recv.at[c],
            {"exp": peer},
        )

    def n_start(c, _):
        def one(s, _):
            n_copy(c, s, ex, (ex + s) % n_exp).start()
            return 0

        lax.fori_loop(1, n_exp, one, 0)
        return 0

    lax.fori_loop(0, chunks, n_start, 0)

    half = steps // 2

    def gather(kind, c, at, where):
        ref = xall.at[(c, *at)]
        return remote(ref, ref, a_send.at[kind], a_recv.at[min(kind, 3), c], where)

    def a_own(c):
        return [gather(0, c, (k, x, y), where) for where in (up, down, far)]

    def a_pass(c):
        return [gather(1, c, (k, 1 - x, y), where) for where in (up, down, far)]

    def a_block(c):
        return gather(2, c, (k, x, y), across)

    def a_plane(c):
        ref = xall.at[c, k, x]
        return remote(ref, ref, a_send.at[4], a_recv.at[2, c], across)

    def a_sib(c, plane):
        return gather(3, c, (k, plane), sib)

    three = pl.ds(0, 3)

    def reduce(kind, c, src, dst, where):
        return remote(src, dst, r_send.at[kind], r_recv.at[kind, c], where)

    def r_sib(c):
        return reduce(0, c, tbuf.at[c, 1 - k], sbuf.at[c], sib)

    def r_pairs(c):
        return (
            reduce(1, c, tbuf.at[c, k, :, y_up], ybuf.at[c // 2, 0], up),
            reduce(1, c, tbuf.at[c, k, :, y_down], ybuf.at[c // 2, 1], down),
            reduce(1, c, tbuf.at[c, k, :, y_far], ybuf.at[c // 2, 2], far),
        )

    def r_block(c):
        return reduce(2, c, tbuf.at[c, k, 1 - x, y], fbuf.at[c, 0], across)

    def r_plane(c):
        return reduce(3, c, tbuf.at[c, k, 1 - x], xbuf.at[c // 2], across)

    def r_own(c):
        return (
            reduce(4, c, tbuf.at[c, k, x, y_up], fbuf.at[c, 0], up),
            reduce(4, c, tbuf.at[c, k, x, y_down], fbuf.at[c, 1], down),
            reduce(4, c, tbuf.at[c, k, x, y_far], fbuf.at[c, 2], far),
        )

    def e_copy(c, s, row_of, slot, peer):
        at = pl.ds(pl.multiple_of(row_of * sub, sub), sub)
        return remote(
            wsend.at[at, cols(c)],
            wrecv.at[slot, :, cols(c)],
            e_send,
            e_recv.at[c],
            {"exp": peer},
        )

    def wave_rows(i):
        return pl.ds(pl.multiple_of(i // chunks * part, part), part)

    def step(it, _):
        @pl.when(it < chunks)
        def _():
            arrived(nbuf.at[pl.ds(0, (n_exp - 1) * sub), cols(it)], n_recv.at[it])

        @pl.when(it < steps)
        def _():
            i = it
            xall[i, k, x, y] = jnp.dot(
                sel_v[wave_rows(i), :], nbuf[:, cols(i % chunks)], preferred_element_type=F32
            ).astype(BF16)

            @pl.when(i % 2 == 0)
            def _():
                a_block(i).start()

            for copy in a_own(i):
                copy.start()

        @pl.when((it >= 2) & (it < steps + 2))
        def _():
            i = it - 2

            @pl.when(i % 2 == 0)
            def _():
                arrived(xall.at[i, k, 1 - x, y], a_recv.at[2, i])
                for copy in a_pass(i):
                    copy.start()
                arrived(xall.at[i, k, x, three], a_recv.at[0, i])

            @pl.when(i % 2 == 1)
            def _():
                arrived(xall.at[i, k, x, three], a_recv.at[0, i])
                a_plane(i).start()

            a_sib(i, x).start()

        @pl.when((it >= 4) & (it < steps + 4))
        def _():
            i = it - 4

            @pl.when(i % 2 == 0)
            def _():
                arrived(xall.at[i, k, 1 - x, three], a_recv.at[1, i])

            @pl.when(i % 2 == 1)
            def _():
                arrived(xall.at[i, k, 1 - x], a_recv.at[2, i])

            a_sib(i, 1 - x).start()

        r = it - (chunks + 5)

        @pl.when((r >= 1) & (r < steps + 1))
        def _():
            i = r - 1
            arrived(sbuf.at[i], r_recv.at[0, i])
            tbuf[i, k] = (tbuf[i, k].astype(F32) + sbuf[i].astype(F32)).astype(BF16)

            @pl.when(i % 2 == 0)
            def _():
                for copy in r_pairs(i):
                    copy.start()

            @pl.when(i % 2 == 1)
            def _():
                r_plane(i).start()

        @pl.when((r >= 3) & (r < steps + 3))
        def _():
            i = r - 3

            @pl.when(i % 2 == 0)
            def _():
                arrived(ybuf.at[i // 2], r_recv.at[1, i])
                for px in range(2):
                    value = tbuf[i, k, px, y].astype(F32)
                    for j in range(3):
                        value = value + ybuf[i // 2, j, px].astype(F32)
                    tbuf[i, k, px, y] = value.astype(BF16)
                r_block(i).start()

            @pl.when(i % 2 == 1)
            def _():
                arrived(xbuf.at[i // 2], r_recv.at[3, i])
                tbuf[i, k, x] = (tbuf[i, k, x].astype(F32) + xbuf[i // 2].astype(F32)).astype(BF16)
                for copy in r_own(i):
                    copy.start()

        @pl.when((r >= 5) & (r < steps + 5))
        def _():
            i = r - 5
            c = i % chunks

            @pl.when(i % 2 == 0)
            def _():
                arrived(fbuf.at[i, 0], r_recv.at[2, i])
                value = tbuf[i, k, x, y].astype(F32) + fbuf[i, 0].astype(F32)
                tbuf[i, k, x, y] = value.astype(BF16)

            @pl.when(i % 2 == 1)
            def _():
                arrived(fbuf.at[i], r_recv.at[4, i])
                value = tbuf[i, k, x, y].astype(F32)
                for j in range(3):
                    value = value + fbuf[i, j].astype(F32)
                tbuf[i, k, x, y] = value.astype(BF16)

            scaled = slot_gate[wave_rows(i), :] * tbuf[i, k, x, y].astype(F32)
            dbuf[wave_rows(i), cols(c)] = scaled.astype(BF16)

            @pl.when(i >= steps - chunks)
            def _():
                wsend[:, cols(c)] = jnp.dot(
                    back_v[...], dbuf[:, cols(c)], preferred_element_type=F32
                ).astype(BF16)

                def start(s, _):
                    peer = (ex + s) % n_exp
                    e_copy(c, s, peer, ex, peer).start()
                    return 0

                lax.fori_loop(1, n_exp, start, 0)
                wrecv[ex, :, cols(c)] = wsend[own_rows, cols(c)]

        @pl.when(r >= steps - chunks + 7)
        def _():
            c = (r - 7) % chunks
            arrived(wsend.at[pl.ds(0, (n_exp - 1) * sub), cols(c)], e_recv.at[c])
            value = mixed_v[:, cols(c)]
            for j in range(n_exp):
                value = value + wrecv[j, :, cols(c)].astype(F32)
            out_ref[:, cols(c)] = value.astype(BF16)

        @pl.when(r == 0)
        def _():
            wd_copy.wait()

        @pl.when((r >= 0) & (r < steps))
        def _():
            i = r
            tbuf[i] = (
                jnp.dot(hid[...], wd_v[:, cols(i % chunks)], preferred_element_type=F32)
                .astype(BF16)
                .reshape(2, 2, n_y, part, span)
            )
            r_sib(i).start()

        @pl.when((it >= 5) & (it < chunks + 5))
        def _():
            for copy in w_copies(it - 5):
                copy.wait()

        @pl.when((it >= 5) & (it < steps + 5))
        def _():
            i = it - 5
            c = i % chunks
            arrived(xall.at[i, 1 - k], a_recv.at[3, i])

            @pl.when(c == 0)
            def _():
                acc_g[...] = jnp.zeros_like(acc_g)
                acc_u[...] = jnp.zeros_like(acc_u)

            lhs = xall[i].reshape(total // waves, span)
            acc_g[...] += jnp.dot(lhs, wg_v[cols(c), :], preferred_element_type=F32)
            acc_u[...] += jnp.dot(lhs, wu_v[cols(c), :], preferred_element_type=F32)

            @pl.when(c == chunks - 1)
            def _():
                gate = acc_g[...]
                hid[...] = (gate / (1.0 + jnp.exp(-gate)) * acc_u[...]).astype(BF16)

        return 0

    lax.fori_loop(0, steps + chunks + 12, step, 0)

    few = pl.ds(0, half)
    for i, ref in enumerate(
        [
            xall.at[:, 0, 0, three],
            xall.at[few, 0, 0, three],
            xall.at[few, 0, 0, 0],
            xall.at[:, 0],
            xall.at[few, 0, 0],
        ]
    ):
        arrived(ref, a_send.at[i])
    for i, ref in enumerate([sbuf, ybuf, fbuf.at[few, 0], xbuf, fbuf.at[few]]):
        arrived(ref, r_send.at[i])
    others = pl.ds(0, (n_exp - 1) * sub)
    arrived(nbuf.at[others], n_send)
    arrived(wsend.at[others], e_send)


def layer_kernel(
    n_ctx,
    n_exp,
    chunks,
    waves,
    cap,
    limit_ref,
    q_ref,
    nk_ref,
    nv_ref,
    ck_ref,
    cv_ref,
    res_ref,
    ow_ref,
    gain_ref,
    wg_ref,
    wu_ref,
    wd_ref,
    ids_ref,
    gates_ref,
    out_ref,
    kbuf,
    vbuf,
    kt,
    vext,
    qbuf,
    osend,
    orecv,
    ssend,
    srecv,
    att,
    psend,
    precv,
    res_v,
    gain_v,
    in_sem,
    kv_send,
    kv_recv,
    q_send,
    q_recv,
    o_send,
    o_recv,
    s_send,
    s_recv,
    p_send,
    p_recv,
    ow_sem,
    normed_v,
    nbuf,
    sel_v,
    back_v,
    slot_gate,
    mixed_v,
    xall,
    wg_v,
    wu_v,
    wd_v,
    acc_g,
    acc_u,
    hid,
    tbuf,
    sbuf,
    dbuf,
    ybuf,
    xbuf,
    fbuf,
    wsend,
    wrecv,
    n_send,
    n_recv,
    a_send,
    a_recv,
    r_send,
    r_recv,
    e_send,
    e_recv,
    wg_sem,
    wu_sem,
    wd_sem,
):
    span = wg_ref.shape[0] // chunks

    def w_copies(c):
        at = pl.ds(pl.multiple_of(c * span, span), span)
        return (
            pltpu.make_async_copy(wg_ref.at[at], wg_v.at[at], wg_sem.at[c]),
            pltpu.make_async_copy(wu_ref.at[at], wu_v.at[at], wu_sem.at[c]),
        )

    def load_weights():
        def one(c, _):
            for copy in w_copies(c):
                copy.start()
            return 0

        lax.fori_loop(0, chunks, one, 0)

    def prepare():
        select_slots(ids_ref, gates_ref, sel_v, back_v, slot_gate)

    ow_v = wd_v.at[pl.ds(0, ow_ref.shape[0])]
    drain = attend_kernel(
        n_ctx,
        n_exp,
        limit_ref,
        q_ref,
        nk_ref,
        nv_ref,
        ck_ref,
        cv_ref,
        res_ref,
        ow_ref,
        gain_ref,
        normed_v,
        mixed_v,
        prepare,
        load_weights,
        kbuf,
        vbuf,
        kt,
        vext,
        qbuf,
        osend,
        orecv,
        ssend,
        srecv,
        att,
        ow_v,
        psend,
        precv,
        res_v,
        gain_v,
        in_sem,
        kv_send,
        kv_recv,
        q_send,
        q_recv,
        o_send,
        o_recv,
        s_send,
        s_recv,
        p_send,
        p_recv,
        ow_sem,
    )
    wd_copy = pltpu.make_async_copy(wd_ref, wd_v, wd_sem)
    wd_copy.start()
    expert_kernel(
        n_ctx,
        n_exp,
        chunks,
        waves,
        cap,
        w_copies,
        wd_copy,
        normed_v,
        out_ref,
        nbuf,
        sel_v,
        back_v,
        slot_gate,
        mixed_v,
        xall,
        wg_v,
        wu_v,
        wd_v,
        acc_g,
        acc_u,
        hid,
        tbuf,
        sbuf,
        dbuf,
        ybuf,
        xbuf,
        fbuf,
        wsend,
        wrecv,
        n_send,
        n_recv,
        a_send,
        a_recv,
        r_send,
        r_recv,
        e_send,
        e_recv,
    )
    drain()


def layer(limit, q, nk, nv, ck, cv, res, ow, gain, wg, wu, wd, ids, gates):
    n_ctx, n_exp = lax.axis_size("ctx"), lax.axis_size("exp")
    n_chip, n_y = n_ctx // 2, n_ctx // 4
    tok, q_width = q.shape
    cache = ck.shape[0]
    sub, width = res.shape
    rows = 2 * (cache + tok)
    block = (q_width // HD) * tok
    hidden = wg.shape[1]
    cap = 3 * tok // n_exp
    chunks, waves = 4, 3
    steps, part = chunks * waves, cap // waves
    span = width // chunks
    total = n_ctx * cap
    vmem = pl.BlockSpec(memory_space=pltpu.VMEM)
    hbm = pl.BlockSpec(memory_space=pl.ANY)
    dma = pltpu.SemaphoreType.DMA
    return pl.pallas_call(
        functools.partial(layer_kernel, n_ctx, n_exp, chunks, waves, cap),
        out_shape=jax.ShapeDtypeStruct((sub, width), BF16),
        in_specs=[pl.BlockSpec(memory_space=pltpu.SMEM)] + [hbm] * 11 + [vmem] * 2,
        out_specs=vmem,
        scratch_shapes=[
            pltpu.VMEM((rows, HD), BF16),
            pltpu.VMEM((rows, HD), BF16),
            pltpu.VMEM((HD, rows), BF16),
            pltpu.VMEM((rows, 2 * HD), BF16),
            pltpu.VMEM((n_chip, block, HD), BF16),
            pltpu.VMEM((n_chip, block, HD), BF16),
            pltpu.VMEM((n_chip, block, HD), BF16),
            pltpu.VMEM((n_chip, 8, tok), F32),
            pltpu.VMEM((n_chip, 8, tok), F32),
            pltpu.VMEM((tok, q_width), BF16),
            pltpu.VMEM((tok, width), BF16),
            pltpu.VMEM((n_exp, sub, width), BF16),
            pltpu.VMEM((sub, width), BF16),
            pltpu.VMEM((1, width), BF16),
            dma((q_width // HD + 6,)),
            dma((4,)),
            dma((4,)),
            dma,
            dma((n_chip,)),
            dma,
            dma,
            dma,
            dma,
            dma,
            dma((2,)),
            dma,
            pltpu.VMEM((sub, width), BF16),
            pltpu.VMEM((tok, width), BF16),
            pltpu.VMEM((cap, tok), BF16),
            pltpu.VMEM((tok, cap), BF16),
            pltpu.VMEM((cap, 1), F32),
            pltpu.VMEM((sub, width), F32),
            pltpu.VMEM((steps, 2, 2, n_y, part, span), BF16),
            pltpu.VMEM((width, hidden), BF16),
            pltpu.VMEM((width, hidden), BF16),
            pltpu.VMEM((hidden, width), BF16),
            pltpu.VMEM((total // waves, hidden), F32),
            pltpu.VMEM((total // waves, hidden), F32),
            pltpu.VMEM((total // waves, hidden), BF16),
            pltpu.VMEM((steps, 2, 2, n_y, part, span), BF16),
            pltpu.VMEM((steps, 2, n_y, part, span), BF16),
            pltpu.VMEM((cap, width), BF16),
            pltpu.VMEM((steps // 2, 3, 2, part, span), BF16),
            pltpu.VMEM((steps // 2, n_y, part, span), BF16),
            pltpu.VMEM((steps, 3, part, span), BF16),
            pltpu.VMEM((tok, width), BF16),
            pltpu.VMEM((n_exp, sub, width), BF16),
            dma,
            dma((chunks,)),
            dma((5,)),
            dma((4, steps)),
            dma((5,)),
            dma((5, steps)),
            dma,
            dma((chunks,)),
            dma((chunks,)),
            dma((chunks,)),
            dma,
        ],
        compiler_params=pltpu.CompilerParams(
            collective_id=0, has_side_effects=True, vmem_limit_bytes=60 * 2**20
        ),
        cost_estimate=pl.CostEstimate(
            flops=6 * total * width * hidden + 4 * n_chip * block * rows * HD,
            bytes_accessed=6 * width * hidden,
            transcendentals=total * hidden + n_chip * block * rows,
        ),
    )(limit, q, nk, nv, ck, cv, res, ow, gain, wg, wu, wd, ids, gates)


def local(
    queries,
    new_keys,
    new_values,
    cache_keys,
    cache_values,
    cache_length,
    residual,
    out_weight,
    norm_gain,
    route_ids,
    route_gates,
    w_gate,
    w_up,
    w_down,
):
    return layer(
        cache_length,
        queries,
        new_keys,
        new_values,
        cache_keys,
        cache_values,
        residual,
        out_weight,
        norm_gain[None, :],
        w_gate[0],
        w_up[0],
        w_down[0],
        route_ids.T,
        route_gates.T,
    )


def solution(mesh):
    placed = (
        P("ctx", "exp"),
        P("ctx", "exp"),
        P("ctx", "exp"),
        P("ctx", "exp"),
        P("ctx", "exp"),
        P(),
        P(("ctx", "exp"), None),
        P("exp", None),
        P(),
        P("ctx", None),
        P("ctx", None),
        P("exp", None, "ctx"),
        P("exp", None, "ctx"),
        P("exp", "ctx", None),
    )
    return jax.shard_map(
        local, mesh=mesh, in_specs=placed, out_specs=P(("ctx", "exp"), None), check_vma=False
    )
```

time: 153 us -> 145 us (0.948)
  Pallas kernels: 149 us -> 142 us
    pallas_call x2 -> x1, Pallas kernels: 149 us -> 142 us  [layer(): pl.pallas_call(functools.partial(layer_kernel, n_ctx, n_exp, chunks, wave...]
where the time goes in v5:
time: 145 us
  Pallas kernels  142 us (98%)
  local copies, waits for them, and re-layouts  2.88 us (2%)
    pallas_call x1, Pallas kernels, layer(): pl.pallas_call(functools.partial(layer_kernel, n_ctx, n_exp, chunks, wave...  142 us

profile of v5, /device:TPU:0, one launch (start us, length us, event | category | flops | bytes accessed | tf_op | source)
XLA Modules:
  0.0 145.1 jit_solution(15854459755464001939)
XLA Ops:
  0.7 1.3 broadcast_in_dim.3.gain_ref
  2.0 141.5 %shard_map.136 = bf16[16,4096]{1,0:T(8,128)(2,1)} custom-call(s32[1]{0:T(128)S(6)} %copy.16.limit_ref, bf16[128,512]{1,0:T(8,128)(2,1)} %q_ref.1, bf16[128,128]{1,0:T(8,128)(2,1)} %nk_ref.1, bf16[128,128]{1,0:T(8,128)(2,1)} %nv_ref.1, bf16[1024,128]{1,0:T(8,128)(2,1)} %ck_ref.1, bf16[1024,128]{1,0:T(8,128)(2,1)} %cv_ref.1, bf16[16,4096]{1,0:T(8,128)(2,1)} %res_ref.1, ...), custom_call_target="tpu_custom_call" | custom-call | flops 21743271936 | bytes 22020096 | tf_op jit(solution)/shard_map/pallas_call | solution.py:865
  143.5 1.6 %copy.17 = bf16[16,4096]{1,0:T(8,128)(2,1)} copy(bf16[16,4096]{1,0:T(8,128)(2,1)} %shard_map.136) | data formatting | bytes 262144

commit v6 on v5

--- a/solution.py
+++ b/solution.py
@@ -279,7 +279,7 @@
 
     mixed = mixed_ref[...]
     square = jnp.mean(mixed * mixed, axis=1, keepdims=True)
-    normed_ref[...] = (mixed * lax.rsqrt(square + EPS) * gain_v[...].astype(F32)).astype(BF16)
+    normed_ref[...] = (mixed * lax.rsqrt(square + EPS) * gain_v[...].reshape(1, width).astype(F32)).astype(BF16)
 
     def drain():
         for copy in kv_copies:
@@ -480,9 +480,9 @@
             for copy in a_own(i):
                 copy.start()
 
-        @pl.when((it >= 2) & (it < steps + 2))
-        def _():
-            i = it - 2
+        @pl.when((it >= 3) & (it < steps + 3))
+        def _():
+            i = it - 3
 
             @pl.when(i % 2 == 0)
             def _():
@@ -498,9 +498,9 @@
 
             a_sib(i, x).start()
 
-        @pl.when((it >= 4) & (it < steps + 4))
-        def _():
-            i = it - 4
+        @pl.when((it >= 6) & (it < steps + 6))
+        def _():
+            i = it - 6
 
             @pl.when(i % 2 == 0)
             def _():
@@ -512,7 +512,7 @@
 
             a_sib(i, 1 - x).start()
 
-        r = it - (chunks + 5)
+        r = it - (chunks + 7)
 
         @pl.when((r >= 1) & (r < steps + 1))
         def _():
@@ -529,9 +529,9 @@
             def _():
                 r_plane(i).start()
 
-        @pl.when((r >= 3) & (r < steps + 3))
-        def _():
-            i = r - 3
+        @pl.when((r >= 4) & (r < steps + 4))
+        def _():
+            i = r - 4
 
             @pl.when(i % 2 == 0)
             def _():
@@ -550,9 +550,9 @@
                 for copy in r_own(i):
                     copy.start()
 
-        @pl.when((r >= 5) & (r < steps + 5))
-        def _():
-            i = r - 5
+        @pl.when((r >= 7) & (r < steps + 7))
+        def _():
+            i = r - 7
             c = i % chunks
 
             @pl.when(i % 2 == 0)
@@ -586,9 +586,9 @@
                 lax.fori_loop(1, n_exp, start, 0)
                 wrecv[ex, :, cols(c)] = wsend[own_rows, cols(c)]
 
-        @pl.when(r >= steps - chunks + 7)
-        def _():
-            c = (r - 7) % chunks
+        @pl.when(r >= steps - chunks + 9)
+        def _():
+            c = (r - 9) % chunks
             arrived(wsend.at[pl.ds(0, (n_exp - 1) * sub), cols(c)], e_recv.at[c])
             value = mixed_v[:, cols(c)]
             for j in range(n_exp):
@@ -609,14 +609,14 @@
             )
             r_sib(i).start()
 
-        @pl.when((it >= 5) & (it < chunks + 5))
-        def _():
-            for copy in w_copies(it - 5):
+        @pl.when((it >= 7) & (it < chunks + 7))
+        def _():
+            for copy in w_copies(it - 7):
                 copy.wait()
 
-        @pl.when((it >= 5) & (it < steps + 5))
-        def _():
-            i = it - 5
+        @pl.when((it >= 7) & (it < steps + 7))
+        def _():
+            i = it - 7
             c = i % chunks
             arrived(xall.at[i, 1 - k], a_recv.at[3, i])
 
@@ -636,7 +636,7 @@
 
         return 0
 
-    lax.fori_loop(0, steps + chunks + 12, step, 0)
+    lax.fori_loop(0, steps + chunks + 16, step, 0)
 
     few = pl.ds(0, half)
     for i, ref in enumerate(
@@ -881,7 +881,7 @@
             pltpu.VMEM((tok, width), BF16),
             pltpu.VMEM((n_exp, sub, width), BF16),
             pltpu.VMEM((sub, width), BF16),
-            pltpu.VMEM((1, width), BF16),
+            pltpu.VMEM((width,), BF16),
             dma((q_width // HD + 6,)),
             dma((4,)),
             dma((4,)),
@@ -963,7 +963,7 @@
         cache_values,
         residual,
         out_weight,
-        norm_gain[None, :],
+        norm_gain,
         w_gate[0],
         w_up[0],
         w_down[0],

time: 145 us -> 140 us (0.966)
  Pallas kernels: 142 us -> 137 us
    pallas_call x1, Pallas kernels: 142 us -> 137 us  [layer(): pl.pallas_call(functools.partial(layer_kernel, n_ctx, n_exp, chunks, wave...]
where the time goes in v6:
time: 140 us
  Pallas kernels  137 us (98%)
  local copies, waits for them, and re-layouts  1.57 us (1%)
    pallas_call x1, Pallas kernels, layer(): pl.pallas_call(functools.partial(layer_kernel, n_ctx, n_exp, chunks, wave...  137 us

profile of v6, /device:TPU:0, one launch (start us, length us, event | category | flops | bytes accessed | tf_op | source)
XLA Modules:
  0.0 139.6 jit_solution(4972130816338783801)
XLA Ops:
  0.7 137.4 %shard_map.136 = bf16[16,4096]{1,0:T(8,128)(2,1)} custom-call(s32[1]{0:T(128)S(6)} %copy.16.limit_ref, bf16[128,512]{1,0:T(8,128)(2,1)} %q_ref.1, bf16[128,128]{1,0:T(8,128)(2,1)} %nk_ref.1, bf16[128,128]{1,0:T(8,128)(2,1)} %nv_ref.1, bf16[1024,128]{1,0:T(8,128)(2,1)} %ck_ref.1, bf16[1024,128]{1,0:T(8,128)(2,1)} %cv_ref.1, bf16[16,4096]{1,0:T(8,128)(2,1)} %res_ref.1, ...), custom_call_target="tpu_custom_call" | custom-call | flops 21743271936 | bytes 22020096 | tf_op jit(solution)/shard_map/pallas_call | solution.py:865
  138.0 1.6 %copy.17 = bf16[16,4096]{1,0:T(8,128)(2,1)} copy(bf16[16,4096]{1,0:T(8,128)(2,1)} %shard_map.136) | data formatting | bytes 262144
